TPU v7x, 32 devices: a whole 2x2x4 slice. The times are simulated.
32 devices in a mesh: kv: 4 (over x, core), seq: 4 (over z), exp: 2 (over y).
Axes of the slice: x: 2, y: 2, z: 4, core: 2. Of those that a mesh axis runs over, the one named last changes fastest.
Arguments:
- queries: bfloat16 [16, 64, 2048], P(('kv', 'seq')), may hold values from -8 to 8
- draft_kv: bfloat16 [2, 16, 64, 2048], P(None, ('kv', 'seq'), 'exp'), may hold values from -12 to 12
- kv_pool: bfloat16 [2, 384, 16, 2048], P(None, ('kv', 'seq', 'exp')), may hold values from -12 to 12
- page_table: int32 [16, 12, 2], P(('kv', 'seq'), None, 'exp'), may hold values from 0 to 11, as said below
- cache_lens: int32 [16], P(('kv', 'seq')), may hold values from 1 to 384, as said below
- parents: int32 [16, 64], P(('kv', 'seq')), may hold values from -1 to 62, as said below
- hidden: bfloat16 [16, 64, 2048], P(('kv', 'seq')), may hold values from -36 to 36
- norm_gain: bfloat16 [2048], replicated, may hold values from 0.5 to 1.5
- out_proj: bfloat16 [2048, 2048], P('exp'), may hold values from -0.125 to 0.125
- router: bfloat16 [2048, 64], replicated, may hold values from -0.125 to 0.125
- routes: int32 [16, 64, 8], P(('kv', 'seq')), may hold values from 0 to 63, all different within a row; in each aligned block of 64 rows (0 to 63, 64 to 127, ..., all dimensions but the last counted through in order) at most 16 rows name the same one
- gate_w: bfloat16 [64, 2048, 1024], P(('kv', 'seq'), None, 'exp'), may hold values from -0.125 to 0.125
- up_w: bfloat16 [64, 2048, 1024], P(('kv', 'seq'), None, 'exp'), may hold values from -0.125 to 0.125
- down_w: bfloat16 [64, 1024, 2048], P(('kv', 'seq'), 'exp'), may hold values from -0.1875 to 0.1875
Outputs:
- output: bfloat16 [16, 64, 2048], P(('kv', 'seq'), None, 'exp')
Inputs may be any that keep to these rules, and one draw needn't show every extreme that they name: For one block of 1 request and one page set s, the entries page_table[r, j, s] over the block's requests r and all j are a permutation of 0 .. 11. `cache_lens`: some request has exactly 384 cached positions. parents[r, 0] = -1; for i >= 1, parents[r, i] is an earlier draft position. `routes`: in each aligned block of 64 token rows (the rows of one device, requests in order), no expert is named by more than 16 rows.
All inputs are finite; a program needn't handle non-finite values.
Results may differ from a plain program's by a relative error of at most 0.02.
Values may be sent and summed in bfloat16 or wider, within the bound.
A program may use at most 128 MiB of HBM per device.

v0:
```python
import jax
import jax.numpy as jnp
from jax import lax
from jax.sharding import PartitionSpec as P

D = 2048
H = 16
EXPERTS = 64
TOPK = 8
CAP = 16


NEG_FILL = -1e30
EPS_NORM = 1e-06


def merged(x, axis, combine):
    everything = jax.tree.map(
        lambda part, kind: lax.all_gather(part.astype(kind), axis),
        x,
        (jnp.bfloat16, jnp.bfloat16, jnp.bfloat16),
    )

    def take(k):
        return jax.tree.map(lambda part, own: part[k].astype(own.dtype), everything, x)

    return lax.fori_loop(
        1, lax.axis_size(axis), lambda k, so_far: combine(so_far, take(k)), take(0)
    )


def ancestry(parents, draft_len):
    positions = jnp.arange(draft_len, dtype=jnp.int32)
    linked = (parents[:, :, None] == positions[None, None, :]).astype(jnp.float32)
    linked = linked + jnp.eye(draft_len, dtype=jnp.float32)[None]
    for doubling in range((draft_len - 1).bit_length()):
        linked = jnp.minimum(
            jnp.einsum("nij,njk->nik", linked, linked, precision=lax.Precision.HIGHEST), 1.0
        )
    return linked


def slot_numbers(flat_routes):
    expert_ids = jnp.arange(EXPERTS, dtype=jnp.int32)
    picked = (flat_routes[:, None] == expert_ids[None, :]).astype(jnp.int32)
    earlier = jnp.cumsum(picked, axis=0) - picked
    return flat_routes * CAP + jnp.sum(earlier * picked, axis=1)


def merge_pair(former, latter):
    new_max = jnp.maximum(former[0], latter[0])
    former_scale = jnp.exp(former[0] - new_max)
    latter_scale = jnp.exp(latter[0] - new_max)
    return (
        new_max,
        former[1] * former_scale + latter[1] * latter_scale,
        former[2] * former_scale[..., None] + latter[2] * latter_scale[..., None],
    )


def send_out(outbound):
    return lax.all_to_all(outbound, ("kv", "seq"), split_axis=0, concat_axis=0, tiled=True)


def local(
    queries,
    draft_kv,
    kv_pool,
    page_table,
    cache_lens,
    parents,
    hidden,
    norm_gain,
    out_proj,
    router,
    routes,
    gate_w,
    up_w,
    down_w,
):
    set_count = lax.axis_size("exp")
    my_set = lax.axis_index("exp")
    req_count, draft_len, feature_width = queries.shape
    head_dim = feature_width // H
    head_share = H // set_count
    page_count = page_table.shape[1]
    page_len = kv_pool.shape[2]
    draft_share = draft_kv.shape[2]
    pool_slots = page_table[:, :, 0]
    cache_keys = kv_pool[0][pool_slots].reshape(req_count, page_count * page_len, feature_width)
    cache_values = kv_pool[1][pool_slots].reshape(req_count, page_count * page_len, feature_width)
    page_ids = jnp.arange(page_count, dtype=jnp.int32)[:, None] * set_count + my_set
    positions = (page_ids * page_len + jnp.arange(page_len, dtype=jnp.int32)[None, :]).reshape(-1)
    cache_seen = positions[None, :] < cache_lens[:, None]
    linked = ancestry(parents, draft_len)
    draft_seen = lax.dynamic_slice_in_dim(linked, my_set * draft_share, draft_share, 2) > 0.5
    visible = jnp.concatenate(
        [
            jnp.broadcast_to(cache_seen[:, None, :], (req_count, draft_len, page_count * page_len)),
            draft_seen,
        ],
        axis=2,
    )
    key_rows = jnp.concatenate([cache_keys, draft_kv[0]], axis=1).reshape(
        req_count, -1, H, head_dim
    )
    value_rows = jnp.concatenate([cache_values, draft_kv[1]], axis=1).reshape(
        req_count, -1, H, head_dim
    )
    query_rows = queries.reshape(req_count, draft_len, H, head_dim)
    scores = jnp.einsum(
        "rqhd,rkhd->rhqk", query_rows, key_rows, preferred_element_type=jnp.float32
    ) * head_dim ** (-0.5)
    scores = jnp.where(visible[:, None], scores, NEG_FILL)
    row_max = jnp.max(scores, axis=3)
    weights = jnp.where(visible[:, None], jnp.exp(scores - row_max[..., None]), 0.0)
    row_sum = jnp.sum(weights, axis=3)
    weighted = jnp.einsum(
        "rhqk,rkhd->rqhd",
        weights.astype(jnp.bfloat16),
        value_rows,
        preferred_element_type=jnp.float32,
    )
    row_max = jnp.transpose(row_max, (0, 2, 1))
    row_sum = jnp.transpose(row_sum, (0, 2, 1))
    row_max, row_sum, weighted = merged((row_max, row_sum, weighted), "exp", merge_pair)
    attended = (weighted / row_sum[..., None]).astype(jnp.bfloat16)
    attended = lax.dynamic_slice_in_dim(attended, my_set * head_share, head_share, 2)
    token_rows = req_count * draft_len
    attended = attended.reshape(token_rows, head_share * head_dim)
    partial_value = jnp.dot(attended, out_proj, preferred_element_type=jnp.float32)
    projected = lax.psum(partial_value.astype(jnp.bfloat16), "exp").astype(jnp.float32)
    residual = hidden.reshape(token_rows, D).astype(jnp.float32) + projected
    mean_sq = jnp.mean(residual * residual, axis=1, keepdims=True)
    normed = (
        residual * lax.rsqrt(mean_sq + EPS_NORM) * norm_gain.astype(jnp.float32)[None, :]
    ).astype(jnp.bfloat16)
    logits = jnp.dot(normed, router, preferred_element_type=jnp.float32)
    chosen = routes.reshape(token_rows, TOPK)
    gate_values = jax.nn.sigmoid(jnp.take_along_axis(logits, chosen, axis=1))
    slot_of = slot_numbers(chosen.reshape(-1)).reshape(token_rows, TOPK)
    slot_ids = jnp.arange(EXPERTS * CAP, dtype=jnp.int32)
    onehot = jnp.any(slot_of[None, :, :] == slot_ids[:, None, None], axis=2).astype(jnp.bfloat16)
    kv_count = lax.axis_size("kv")
    seq_count = lax.axis_size("seq")
    source_count = kv_count * seq_count
    local_experts = gate_w.shape[0]
    column_count = D // set_count
    buffer = jnp.dot(onehot, normed, preferred_element_type=jnp.float32).astype(jnp.bfloat16)
    received = send_out(buffer.reshape(source_count, local_experts, CAP, D))
    gate_pre = jnp.einsum("secd,edf->secf", received, gate_w, preferred_element_type=jnp.float32)
    up_pre = jnp.einsum("secd,edf->secf", received, up_w, preferred_element_type=jnp.float32)
    activity = (jax.nn.silu(gate_pre) * up_pre).astype(jnp.bfloat16)
    finished = jnp.einsum(
        "secf,efd->secd", activity, down_w, preferred_element_type=jnp.float32
    ).astype(jnp.bfloat16)
    returned = lax.all_to_all(finished, ("kv", "seq"), split_axis=0, concat_axis=0, tiled=True)
    flat_back = returned.reshape(EXPERTS * CAP, D)
    combined = jnp.zeros((token_rows, D), jnp.float32)
    for pick_index in range(TOPK):
        combined = combined + gate_values[:, pick_index : pick_index + 1] * flat_back[
            slot_of[:, pick_index]
        ].astype(jnp.float32)
    summed_share = lax.psum_scatter(
        combined.astype(jnp.bfloat16), "exp", scatter_dimension=1, tiled=True
    ).astype(jnp.float32)
    own_columns = lax.dynamic_slice_in_dim(residual, my_set * column_count, column_count, 1)
    return (
        (own_columns + summed_share)
        .astype(jnp.bfloat16)
        .reshape(req_count, draft_len, column_count)
    )


def solution(mesh):
    in_specs = (
        P(("kv", "seq"), None, None),
        P(None, ("kv", "seq"), "exp", None),
        P(None, ("kv", "seq", "exp"), None, None),
        P(("kv", "seq"), None, "exp"),
        P(("kv", "seq")),
        P(("kv", "seq"), None),
        P(("kv", "seq"), None, None),
        P(),
        P("exp", None),
        P(),
        P(("kv", "seq"), None, None),
        P(("kv", "seq"), None, "exp"),
        P(("kv", "seq"), None, "exp"),
        P(("kv", "seq"), "exp", None),
    )
    out_specs = P(("kv", "seq"), None, "exp")
    return jax.shard_map(local, mesh=mesh, in_specs=in_specs, out_specs=out_specs, check_vma=False)
```

profile of v0, /device:TPU:0, one launch (start us, length us, event | category | flops | bytes accessed | tf_op | source)
XLA Modules:
  0.0 340.3 jit_solution(3774119205482321948)
XLA Ops:
  7.2 0.7 fusion.66
  8.0 0.1 reshape.596
  8.1 0.8 fusion.56
  8.9 0.2 convolution_minimum_fusion.4
  9.0 0.2 convolution_minimum_fusion.3
  9.2 0.2 convolution_minimum_fusion.2
  9.4 0.2 convolution_minimum_fusion.1
  9.5 0.2 convolution_minimum_fusion
  9.7 0.2 fusion.74
  9.9 1.0 copy.118
  10.9 1.0 slice_bitcast_fusion.3
  12.0 1.5 slice_bitcast_fusion.1
  13.5 0.6 gather_fusion
  14.1 0.6 gather_fusion.1
  14.7 0.2 copy.116
  14.9 0.2 copy.94
  15.1 0.2 copy.119
  15.2 0.2 copy.91
  15.6 0.8 fusion.73
  16.4 0.4 fusion.31
  16.9 0.5 fusion.25
  17.4 0.2 copy.97
  17.6 5.3 %all-gather.2 = bf16[2,64,16]{1,2,0:T(8,128)(2,1)S(1)} all-gather(bf16[1,64,16]{1,2,0:T(8,128)(2,1)S(1)} %bitcast.216), channel_id=4, replica_groups=mesh['kv'=4,'seq'=4,'exp'=2] {'exp'}, dimensions={0}, use_global_device_ids=true | all-gather | bytes 6144 | tf_op jit(solution)/shard_map/all_gather | solution.py:19
  22.8 4.3 %all-gather.1 = bf16[2,64,16]{1,2,0:T(8,128)(2,1)S(1)} all-gather(bf16[1,64,16]{1,2,0:T(8,128)(2,1)S(1)} %convert_bitcast_fusion.2), channel_id=3, replica_groups=mesh['kv'=4,'seq'=4,'exp'=2] {'exp'}, dimensions={0}, use_global_device_ids=true | all-gather | bytes 6144 | tf_op jit(solution)/shard_map/all_gather | solution.py:19
  27.4 7.2 %all-gather = bf16[2,64,16,128]{3,2,1,0:T(8,128)(2,1)S(1)} all-gather(bf16[1,64,16,128]{3,2,1,0:T(8,128)(2,1)S(1)} %copy.97), channel_id=2, replica_groups=mesh['kv'=4,'seq'=4,'exp'=2] {'exp'}, dimensions={0}, use_global_device_ids=true | all-gather | bytes 786432 | tf_op jit(solution)/shard_map/all_gather | solution.py:19
  34.8 0.3 fusion.40
  35.1 3.7 %convolution_convert_fusion.1 = bf16[64,2048]{1,0:T(8,128)(2,1)} fusion(bf16[1024,2048]{1,0:T(8,128)(2,1)} %param.22, bf16[8,8,8,128]{3,2,1,0:T(8,128)(2,1)S(1)} %bitcast.210), kind=kOutput, calls=%fused_computation.21 | convolution fusion | flops 268566528 | bytes 4587520 | tf_op jit(solution)/shard_map/dot_general | solution.py:131
  38.9 0.1 copy.101
  39.0 0.1 eq.105
  39.1 0.1 eq.101
  39.2 1.2 reduce-window.6
  40.4 0.2 slice_reduce_fusion
  40.7 0.1 fusion.46
  40.8 0.1 reduce_sum.34
  41.0 0.1 copy.107
  41.0 0.7 fusion.14
  41.8 22.2 %all-reduce.2.cloned.1.call-done = bf16[64,2048]{1,0:T(8,128)(2,1)} async-done(((bf16[64,2048]{1,0:T(8,128)(2,1)}), bf16[64,2048]{1,0:T(8,128)(2,1)}) %all-reduce.2.cloned.1.call-update) | async-done | bytes 262160 | tf_op jit(solution)/shard_map/psum | solution.py:132
  64.0 1.2 convert_add_fusion
  65.2 2.4 convolution_convert_fusion
  67.6 100.1 %all_to_all.10 = bf16[16,4,16,2048]{3,2,1,0:T(8,128)(2,1)S(1)} all-to-all(bf16[16,4,16,2048]{3,2,1,0:T(8,128)(2,1)S(1)} %bitcast.205), channel_id=1, replica_groups=mesh['kv'=4,'seq'=4,'exp'=2] {'kv','seq'}, dimensions={0} | all-to-all | bytes 8388608 | tf_op jit(solution)/shard_map/all_to_all | solution.py:62
  167.8 2.0 copy-done.1
  169.8 3.7 %fusion.4 = f32[4,16,16,512]{3,2,1,0:T(8,128)} fusion(bf16[4,2048,512]{2,1,0:T(8,128)(2,1)S(1)} %bitcast.219, bf16[16,4,16,2048]{3,2,1,0:T(8,128)(2,1)S(1)} %all_to_all.10), kind=kOutput, calls=%fused_computation.15 | convolution fusion | flops 2147483648 | bytes 14680064 | tf_op jit(solution)/shard_map/secd,edf->secf/dot_general | solution.py:151
  173.5 14.1 %convert_bitcast_fusion = bf16[16,4,16,2048]{3,2,0,1:T(8,128)(2,1)} fusion(bf16[4,512,2048]{2,1,0:T(8,128)(2,1)} %param.27, f32[4,16,16,512]{3,2,1,0:T(8,128)} %fusion.4, bf16[4,2048,512]{2,1,0:T(8,128)(2,1)} %param.26, bf16[16,4,16,2048]{3,2,1,0:T(8,128)(2,1)} %copy-done.1), kind=kOutput, calls=%fused_computation.17 | convolution fusion | flops 4300210176 | bytes 27262976 | tf_op jit(solution)/shard_map/secf,efd->secd/dot_general | solution.py:154
  187.6 4.7 %copy.110 = bf16[16,4,16,2048]{3,2,1,0:T(8,128)(2,1)} copy(bf16[16,4,16,2048]{3,2,0,1:T(8,128)(2,1)} %convert_bitcast_fusion) | data formatting | bytes 8388608 | tf_op jit(solution)/shard_map/convert_element_type | solution.py:156
  192.4 4.7 %all-to-all-start.1 = ((bf16[16,4,16,2048]{3,2,1,0:T(8,128)(2,1)}), bf16[16,4,16,2048]{3,2,1,0:T(8,128)(2,1)}, u32[]{:S(2)}, u32[]{:S(2)}) async-start(bf16[16,4,16,2048]{3,2,1,0:T(8,128)(2,1)} %copy.110), calls=%async_computation.1 | async-start | bytes 8388608 | tf_op jit(solution)/shard_map/all_to_all | solution.py:157
  197.0 0.3 reduce-scatter.2.cloned.1.call-start
  197.4 0.1 copy.102
  197.5 0.1 reshape.547
  197.6 0.3 fusion.48
  198.0 0.3 fusion.71
  198.3 3.8 %gather_fusion.10 = f32[512]{0:T(512)S(1)} fusion(f32[64,64]{1,0:T(8,128)S(1)} %fusion.71, s32[512]{0:T(512)S(1)} %reshape.547), kind=kCustom, calls=%fused_computation.10 | custom fusion | bytes 8192 | tf_op jit(solution)/shard_map/jit(take_along_axis)/gather | solution.py:140
  202.2 0.3 slice_reduce_fusion.8
  202.6 88.9 %all-to-all-done.1 = bf16[16,4,16,2048]{3,2,1,0:T(8,128)(2,1)} async-done(((bf16[16,4,16,2048]{3,2,1,0:T(8,128)(2,1)}), bf16[16,4,16,2048]{3,2,1,0:T(8,128)(2,1)}, u32[]{:S(2)}, u32[]{:S(2)}) %all-to-all-start.1) | async-done | bytes 4194336 | tf_op jit(solution)/shard_map/all_to_all | solution.py:157
  291.4 3.7 %gather_fusion.9 = bf16[64,2048]{1,0:T(8,128)(2,1)S(1)} fusion(bf16[1024,2048]{1,0:T(8,128)(2,1)} %bitcast.38, s32[1024]{0:T(1024)S(1)} %get-tuple-element.60), kind=kCustom, calls=%fused_computation.9 | custom fusion | bytes 524544 | tf_op jit(solution)/shard_map/gather | solution.py:161
  295.1 3.7 %gather_fusion.8 = bf16[64,2048]{1,0:T(8,128)(2,1)S(1)} fusion(bf16[1024,2048]{1,0:T(8,128)(2,1)} %bitcast.38, s32[1024]{0:T(1024)S(1)} %get-tuple-element.61), kind=kCustom, calls=%fused_computation.8 | custom fusion | bytes 524544 | tf_op jit(solution)/shard_map/gather | solution.py:161
  298.9 3.7 %gather_fusion.7 = bf16[64,2048]{1,0:T(8,128)(2,1)S(1)} fusion(bf16[1024,2048]{1,0:T(8,128)(2,1)} %bitcast.38, s32[1024]{0:T(1024)S(1)} %get-tuple-element.62), kind=kCustom, calls=%fused_computation.7 | custom fusion | bytes 524544 | tf_op jit(solution)/shard_map/gather | solution.py:161
  302.6 3.7 %gather_fusion.6 = bf16[64,2048]{1,0:T(8,128)(2,1)S(1)} fusion(bf16[1024,2048]{1,0:T(8,128)(2,1)} %bitcast.38, s32[1024]{0:T(1024)S(1)} %get-tuple-element.63), kind=kCustom, calls=%fused_computation.6 | custom fusion | bytes 524544 | tf_op jit(solution)/shard_map/gather | solution.py:161
  306.3 3.7 %gather_fusion.5 = bf16[64,2048]{1,0:T(8,128)(2,1)S(1)} fusion(bf16[1024,2048]{1,0:T(8,128)(2,1)} %bitcast.38, s32[1024]{0:T(1024)S(1)} %get-tuple-element.64), kind=kCustom, calls=%fused_computation.5 | custom fusion | bytes 524544 | tf_op jit(solution)/shard_map/gather | solution.py:161
  310.0 3.7 %gather_fusion.4 = bf16[64,2048]{1,0:T(8,128)(2,1)S(1)} fusion(bf16[1024,2048]{1,0:T(8,128)(2,1)} %bitcast.38, s32[1024]{0:T(1024)S(1)} %get-tuple-element.65), kind=kCustom, calls=%fused_computation.4 | custom fusion | bytes 524544 | tf_op jit(solution)/shard_map/gather | solution.py:161
  313.7 3.7 %gather_fusion.3 = bf16[64,2048]{1,0:T(8,128)(2,1)S(1)} fusion(bf16[1024,2048]{1,0:T(8,128)(2,1)} %bitcast.38, s32[1024]{0:T(1024)S(1)} %get-tuple-element.66), kind=kCustom, calls=%fused_computation.3 | custom fusion | bytes 524544 | tf_op jit(solution)/shard_map/gather | solution.py:161
  317.5 3.7 %gather_fusion.2 = bf16[64,2048]{1,0:T(8,128)(2,1)S(1)} fusion(bf16[1024,2048]{1,0:T(8,128)(2,1)} %bitcast.38, s32[1024]{0:T(1024)S(1)} %get-tuple-element.67), kind=kCustom, calls=%fused_computation.2 | custom fusion | bytes 524544 | tf_op jit(solution)/shard_map/gather | solution.py:161
  321.2 1.2 add_convert_fusion
  322.4 9.5 %reduce-scatter.2.cloned.1.call-done = bf16[64,1024]{1,0:T(8,128)(2,1)} async-done(((bf16[64,2048]{1,0:T(8,128)(2,1)}), bf16[64,1024]{1,0:T(8,128)(2,1)}) %reduce-scatter.2.cloned.1.call-update) | async-done | bytes 131088 | tf_op jit(solution)/shard_map/reduce_scatter | solution.py:164
  331.9 1.6 fusion.41
  (53 shorter events, 1.3 us)
Async XLA Ops:
  6.5 191.5 %copy-start = (bf16[2048,64]{0,1:T(8,128)(2,1)S(1)}, bf16[2048,64]{0,1:T(8,128)(2,1)}, u32[]{:S(2)}) copy-start(bf16[2048,64]{0,1:T(8,128)(2,1)} %param.23) | copy-start | bytes 786436
  6.5 57.5 %all-reduce.2.cloned.1.call-start = ((), (), s32[]{:S(2)}) async-start(), calls=%async_computation.3 | async-start | bytes 524288 | tf_op jit(solution)/shard_map/psum | solution.py:132
  17.4 21.5 %copy-start.4 = (s32[1,64,8]{1,2,0:T(8,128)S(1)}, s32[1,64,8]{1,2,0:T(8,128)}, u32[]{:S(2)}) copy-start(s32[1,64,8]{1,2,0:T(8,128)} %param.24) | copy-start | bytes 6148
  17.4 21.8 %copy-start.5 = (bf16[2048]{0:T(1024)(128)(2,1)S(1)}, bf16[2048]{0:T(1024)(128)(2,1)}, u32[]{:S(2)}) copy-start(bf16[2048]{0:T(1024)(128)(2,1)} %param.21) | copy-start | bytes 12292
  27.4 36.6 %copy-start.2 = (bf16[1,64,2048]{2,1,0:T(8,128)(2,1)S(1)}, bf16[1,64,2048]{2,1,0:T(8,128)(2,1)}, u32[]{:S(2)}) copy-start(bf16[1,64,2048]{2,1,0:T(8,128)(2,1)} %param.20) | copy-start | bytes 786436
  65.2 104.6 %slice-start = ((s8[8388608]{0:T(1024)(128)(4,1)}), s8[4194304]{0:T(1024)(128)(4,1)S(1)}, s32[]{:S(2)}) async-start(s8[8388608]{0:T(1024)(128)(4,1)} %bitcast.218), calls=%async_computation.5 | async-start | bytes 8388608
  67.6 102.1 %slice-start.1 = ((s8[8388608]{0:T(1024)(128)(4,1)}), s8[4194304]{0:T(1024)(128)(4,1)S(1)}, s32[]{:S(2)}) async-start(s8[8388608]{0:T(1024)(128)(4,1)} %bitcast.218), calls=%async_computation.6 | async-start | bytes 8388608
  167.8 2.0 copy-start.1
  192.4 5.6 %copy-start.3 = (bf16[64,2048]{1,0:T(8,128)(2,1)S(1)}, bf16[64,2048]{1,0:T(8,128)(2,1)}, u32[]{:S(2)}) copy-start(bf16[64,2048]{1,0:T(8,128)(2,1)} %all-reduce.2.cloned.1.call-done) | copy-start | bytes 786436
  192.4 99.0 %all-to-all-start.1 = ((bf16[16,4,16,2048]{3,2,1,0:T(8,128)(2,1)}), bf16[16,4,16,2048]{3,2,1,0:T(8,128)(2,1)}, u32[]{:S(2)}, u32[]{:S(2)}) async-start(bf16[16,4,16,2048]{3,2,1,0:T(8,128)(2,1)} %copy.110), calls=%async_computation.1 | async-start | bytes 8388608 | tf_op jit(solution)/shard_map/all_to_all | solution.py:157
  197.0 134.9 %reduce-scatter.2.cloned.1.call-start = ((), (), s32[]{:S(2)}) async-start(), calls=%async_computation.4 | async-start | bytes 393216 | tf_op jit(solution)/shard_map/reduce_scatter | solution.py:164
Sparse Core Ops, SparseCore 0:
  39.0 24.9 all-reduce.1
  322.5 9.3 reduce-scatter.1
where the time goes:
time: 341 us; the launch traced here: 340 us
  waiting for transfers between devices  121 us (35%)
  blocking collectives  117 us (34%)
  local copies, waits for them, and re-layouts  47.8 us (14%)
  matrix products  26.6 us (8%)
  between operations  14.6 us (4%)
  other arithmetic  8.87 us (3%)
  starting transfers between devices  4.93 us (1%)
    all_to_all x1, blocking collectives, send_out(): lax.all_to_all(outbound, ('kv', 'seq'), split_axis=0, concat_axis=0, tile...  100 us
    all_to_all x1, waiting for transfers between devices, local(): lax.all_to_all(finished, ('kv', 'seq'), split_axis=0, concat_axis=0, tile...  88.9 us
    gather x8, local copies, waits for them, and re-layouts, local(): flat_back[slot_of[:, pick_index]].astype(jnp.float32)  29.7 us
    psum x1, waiting for transfers between devices, local(): lax.psum(partial_value.astype(jnp.bfloat16), 'exp').astype(jnp.float32)  22.2 us
    all_gather x3, blocking collectives, merged(): lax.all_gather(part.astype(kind), axis)  16.8 us
    dot_general x1, matrix products, local(): jnp.einsum('secf,efd->secd', activity, down_w, preferred_element_type=jnp...  14.1 us
    reduce_scatter x1, waiting for transfers between devices, local(): lax.psum_scatter(combined.astype(jnp.bfloat16), 'exp', scatter_dimension=...  9.5 us
  transfers between devices with their start and end apart: 3, of which 3 were waited for; matrix products, arithmetic and copies ran while one was open for 2% of the time, Pallas kernels for 0%

commit v1 on v0

--- a/solution.py
+++ b/solution.py
@@ -40,13 +40,6 @@
     return linked
 
 
-def slot_numbers(flat_routes):
-    expert_ids = jnp.arange(EXPERTS, dtype=jnp.int32)
-    picked = (flat_routes[:, None] == expert_ids[None, :]).astype(jnp.int32)
-    earlier = jnp.cumsum(picked, axis=0) - picked
-    return flat_routes * CAP + jnp.sum(earlier * picked, axis=1)
-
-
 def merge_pair(former, latter):
     new_max = jnp.maximum(former[0], latter[0])
     former_scale = jnp.exp(former[0] - new_max)
@@ -56,10 +49,6 @@
         former[1] * former_scale + latter[1] * latter_scale,
         former[2] * former_scale[..., None] + latter[2] * latter_scale[..., None],
     )
-
-
-def send_out(outbound):
-    return lax.all_to_all(outbound, ("kv", "seq"), split_axis=0, concat_axis=0, tiled=True)
 
 
 def local(
@@ -86,12 +75,17 @@
     page_count = page_table.shape[1]
     page_len = kv_pool.shape[2]
     draft_share = draft_kv.shape[2]
-    pool_slots = page_table[:, :, 0]
-    cache_keys = kv_pool[0][pool_slots].reshape(req_count, page_count * page_len, feature_width)
-    cache_values = kv_pool[1][pool_slots].reshape(req_count, page_count * page_len, feature_width)
-    page_ids = jnp.arange(page_count, dtype=jnp.int32)[:, None] * set_count + my_set
-    positions = (page_ids * page_len + jnp.arange(page_len, dtype=jnp.int32)[None, :]).reshape(-1)
-    cache_seen = positions[None, :] < cache_lens[:, None]
+    slot_ids = jnp.arange(page_count, dtype=jnp.int32)
+    page_of = jnp.sum(
+        jnp.where(page_table[:, :, 0][:, :, None] == slot_ids, slot_ids[None, :, None], 0), axis=1
+    )
+    cache_keys = kv_pool[0].reshape(req_count, page_count * page_len, feature_width)
+    cache_values = kv_pool[1].reshape(req_count, page_count * page_len, feature_width)
+    positions = (
+        (page_of * set_count + my_set)[:, :, None] * page_len
+        + jnp.arange(page_len, dtype=jnp.int32)[None, None, :]
+    ).reshape(req_count, -1)
+    cache_seen = positions < cache_lens[:, None]
     linked = ancestry(parents, draft_len)
     draft_seen = lax.dynamic_slice_in_dim(linked, my_set * draft_share, draft_share, 2) > 0.5
     visible = jnp.concatenate(
@@ -135,35 +129,36 @@
     normed = (
         residual * lax.rsqrt(mean_sq + EPS_NORM) * norm_gain.astype(jnp.float32)[None, :]
     ).astype(jnp.bfloat16)
-    logits = jnp.dot(normed, router, preferred_element_type=jnp.float32)
-    chosen = routes.reshape(token_rows, TOPK)
-    gate_values = jax.nn.sigmoid(jnp.take_along_axis(logits, chosen, axis=1))
-    slot_of = slot_numbers(chosen.reshape(-1)).reshape(token_rows, TOPK)
-    slot_ids = jnp.arange(EXPERTS * CAP, dtype=jnp.int32)
-    onehot = jnp.any(slot_of[None, :, :] == slot_ids[:, None, None], axis=2).astype(jnp.bfloat16)
-    kv_count = lax.axis_size("kv")
-    seq_count = lax.axis_size("seq")
-    source_count = kv_count * seq_count
+    spread = ("kv", "seq")
     local_experts = gate_w.shape[0]
     column_count = D // set_count
-    buffer = jnp.dot(onehot, normed, preferred_element_type=jnp.float32).astype(jnp.bfloat16)
-    received = send_out(buffer.reshape(source_count, local_experts, CAP, D))
-    gate_pre = jnp.einsum("secd,edf->secf", received, gate_w, preferred_element_type=jnp.float32)
-    up_pre = jnp.einsum("secd,edf->secf", received, up_w, preferred_element_type=jnp.float32)
-    activity = (jax.nn.silu(gate_pre) * up_pre).astype(jnp.bfloat16)
+    my_block = lax.axis_index("kv") * lax.axis_size("seq") + lax.axis_index("seq")
+    all_routes = lax.all_gather(routes.reshape(token_rows, TOPK), spread)
+    sources = all_routes.shape[0]
+    expert_ids = my_block * local_experts + jnp.arange(local_experts, dtype=jnp.int32)
+    member = jnp.any(all_routes[:, None] == expert_ids[None, :, None, None], axis=3).astype(jnp.int32)
+    rank = jnp.cumsum(member, axis=2) - member
+    chosen = (member[:, :, None, :] > 0) & (
+        rank[:, :, None, :] == jnp.arange(CAP, dtype=jnp.int32)[None, None, :, None]
+    )
+    chosen = chosen.astype(jnp.bfloat16)
+    all_rows = lax.all_gather(normed, spread)
+    picked = jnp.einsum("sect,std->escd", chosen, all_rows, preferred_element_type=jnp.float32)
+    picked = picked.astype(jnp.bfloat16).reshape(local_experts, sources * CAP, D)
+    own_router = lax.dynamic_slice_in_dim(router, my_block * local_experts, local_experts, 1)
+    logits = jnp.einsum("erd,de->er", picked, own_router, preferred_element_type=jnp.float32)
+    gate_pre = jnp.einsum("erd,edf->erf", picked, gate_w, preferred_element_type=jnp.float32)
+    up_pre = jnp.einsum("erd,edf->erf", picked, up_w, preferred_element_type=jnp.float32)
+    activity = jax.nn.silu(gate_pre) * up_pre * jax.nn.sigmoid(logits)[:, :, None]
     finished = jnp.einsum(
-        "secf,efd->secd", activity, down_w, preferred_element_type=jnp.float32
-    ).astype(jnp.bfloat16)
-    returned = lax.all_to_all(finished, ("kv", "seq"), split_axis=0, concat_axis=0, tiled=True)
-    flat_back = returned.reshape(EXPERTS * CAP, D)
-    combined = jnp.zeros((token_rows, D), jnp.float32)
-    for pick_index in range(TOPK):
-        combined = combined + gate_values[:, pick_index : pick_index + 1] * flat_back[
-            slot_of[:, pick_index]
-        ].astype(jnp.float32)
+        "erf,efd->erd", activity.astype(jnp.bfloat16), down_w, preferred_element_type=jnp.float32
+    ).astype(jnp.bfloat16).reshape(local_experts, sources, CAP, D)
+    combined = jnp.einsum("sect,escd->std", chosen, finished, preferred_element_type=jnp.float32)
+    combined = combined.astype(jnp.bfloat16).reshape(sources, token_rows, set_count, column_count)
+    combined = jnp.transpose(combined, (0, 2, 1, 3)).reshape(-1, token_rows, column_count)
     summed_share = lax.psum_scatter(
-        combined.astype(jnp.bfloat16), "exp", scatter_dimension=1, tiled=True
-    ).astype(jnp.float32)
+        combined, ("kv", "seq", "exp"), scatter_dimension=0, tiled=True
+    )[0].astype(jnp.float32)
     own_columns = lax.dynamic_slice_in_dim(residual, my_set * column_count, column_count, 1)
     return (
         (own_columns + summed_share)

time: 341 us -> 298 us (0.87)
  blocking collectives: 117 us -> 49.3 us
  waiting for transfers between devices: 121 us -> 185 us
  local copies, waits for them, and re-layouts: 47.8 us -> 8.27 us
  starting transfers between devices: 4.93 us -> 0.09 us
  matrix products: 26.6 us -> 30.2 us
    reduce_scatter x1, waiting for transfers between devices: 9.5 us -> 143 us  [local(): lax.psum_scatter(combined, ('kv', 'seq', 'exp'), scatter_dimension=0, til...]
    all_to_all x1 -> x0, blocking collectives: 100 us -> none  [send_out(): lax.all_to_all(outbound, ('kv', 'seq'), split_axis=0, concat_axis=0, tile...]
    all_to_all x1 -> x0, waiting for transfers between devices: 88.9 us -> none  [local(): lax.all_to_all(finished, ('kv', 'seq'), split_axis=0, concat_axis=0, tile...]
    gather x14 -> x0, local copies, waits for them, and re-layouts: 34.9 us -> none  [the longest x8 29.7 us: local(): flat_back[slot_of[:, pick_index]].astype(jnp.float32)]
    all_gather x0 -> x1, blocking collectives: none -> 32.7 us  [local(): all_routes = lax.all_gather(routes.reshape(token_rows, TOPK), spread)]
    all_gather x0 -> x1, waiting for transfers between devices: none -> 17.3 us  [local(): all_rows = lax.all_gather(normed, spread)]
    all_to_all x1 -> x0, starting transfers between devices: 4.66 us -> none  [local(): lax.all_to_all(finished, ('kv', 'seq'), split_axis=0, concat_axis=0, tile...]
    convert_element_type x1, local copies, waits for them, and re-layouts: 4.74 us -> 0.31 us  [local(): picked.astype(jnp.bfloat16).reshape(local_experts, sources * CAP, D)]
  transfers between devices with their start and end apart: 3 -> 3, of which waited for: 3 -> 3; matrix products, arithmetic and copies ran while one was open for 2% -> 0% of each run, Pallas kernels for 0% -> 0%
where the time goes in v1:
time: 298 us
  waiting for transfers between devices  185 us (62%)
  blocking collectives  49.3 us (17%)
  matrix products  30.2 us (10%)
  between operations  14.2 us (5%)
  other arithmetic  10.6 us (4%)
  local copies, waits for them, and re-layouts  8.27 us (3%)
    reduce_scatter x1, waiting for transfers between devices, local(): lax.psum_scatter(combined, ('kv', 'seq', 'exp'), scatter_dimension=0, til...  143 us
    all_gather x1, blocking collectives, local(): all_routes = lax.all_gather(routes.reshape(token_rows, TOPK), spread)  32.7 us
    psum x1, waiting for transfers between devices, local(): lax.psum(partial_value.astype(jnp.bfloat16), 'exp').astype(jnp.float32)  25.1 us
    all_gather x1, waiting for transfers between devices, local(): all_rows = lax.all_gather(normed, spread)  17.3 us
    all_gather x3, blocking collectives, merged(): lax.all_gather(part.astype(kind), axis)  16.6 us
    dot_general x1, matrix products, local(): jnp.einsum('erf,efd->erd', activity.astype(jnp.bfloat16), down_w, preferr...  13.7 us
  transfers between devices with their start and end apart: 3, of which 3 were waited for; matrix products, arithmetic and copies ran while one was open for 0% of the time, Pallas kernels for 0%

profile of v1, /device:TPU:0, one launch (start us, length us, event | category | flops | bytes accessed | tf_op | source)
XLA Modules:
  0.0 297.7 jit_solution(2053729750827698510)
XLA Ops:
  7.2 0.7 fusion.39
  8.0 0.1 broadcast_reduce_fusion
  8.1 0.1 add.150
  8.2 0.1 add.152
  8.3 0.8 fusion.29
  9.1 0.2 convolution_minimum_fusion.4
  9.2 0.2 convolution_minimum_fusion.3
  9.4 0.2 convolution_minimum_fusion.2
  9.6 0.2 convolution_minimum_fusion.1
  9.7 0.2 convolution_minimum_fusion
  9.9 0.2 fusion.51
  10.1 1.0 copy.70
  11.1 1.0 slice_bitcast_fusion.1
  12.2 1.5 fusion.48
  13.8 0.2 copy.71
  13.9 0.2 copy.48
  14.1 0.2 copy.68
  14.3 0.2 copy.51
  14.5 0.1 fusion.33
  14.6 0.1 add_bitcast_fusion
  14.7 0.8 fusion.50
  15.5 0.4 fusion.8
  15.9 0.5 fusion.3
  16.4 0.0 copy-start.4
  16.5 0.0 copy-start.3
  16.5 0.2 copy.54
  16.6 5.3 %all-gather.2 = bf16[2,64,16]{1,2,0:T(8,128)(2,1)S(1)} all-gather(bf16[1,64,16]{1,2,0:T(8,128)(2,1)S(1)} %bitcast.167), channel_id=4, replica_groups=mesh['kv'=4,'seq'=4,'exp'=2] {'exp'}, dimensions={0}, use_global_device_ids=true | all-gather | bytes 6144 | tf_op jit(solution)/shard_map/all_gather | solution.py:19
  21.9 4.3 %all-gather.1 = bf16[2,64,16]{1,2,0:T(8,128)(2,1)S(1)} all-gather(bf16[1,64,16]{1,2,0:T(8,128)(2,1)S(1)} %convert_bitcast_fusion.2), channel_id=3, replica_groups=mesh['kv'=4,'seq'=4,'exp'=2] {'exp'}, dimensions={0}, use_global_device_ids=true | all-gather | bytes 6144 | tf_op jit(solution)/shard_map/all_gather | solution.py:19
  26.2 0.1 copy.55
  26.3 0.1 copy.57
  26.4 0.1 copy.56
  26.5 7.1 %all-gather = bf16[2,64,16,128]{3,2,1,0:T(8,128)(2,1)S(1)} all-gather(bf16[1,64,16,128]{3,2,1,0:T(8,128)(2,1)S(1)} %copy.54), channel_id=2, replica_groups=mesh['kv'=4,'seq'=4,'exp'=2] {'exp'}, dimensions={0}, use_global_device_ids=true | all-gather | bytes 786432 | tf_op jit(solution)/shard_map/all_gather | solution.py:19
  33.6 0.1 constant_dynamic-slice_fusion.2
  33.7 0.1 constant_dynamic-slice_fusion
  33.8 0.3 fusion.21
  34.0 3.7 %convolution_convert_fusion.1 = bf16[64,2048]{1,0:T(8,128)(2,1)} fusion(bf16[1024,2048]{1,0:T(8,128)(2,1)} %param.22, bf16[8,8,8,128]{3,2,1,0:T(8,128)(2,1)S(1)} %bitcast.161), kind=kOutput, calls=%fused_computation.5 | convolution fusion | flops 268566528 | bytes 4587520 | tf_op jit(solution)/shard_map/dot_general | solution.py:125
  37.8 0.0 all-reduce.2.cloned.1.call-update
  37.8 0.0 all-gather.6.cloned.1.call-start
  37.9 25.1 %all-reduce.2.cloned.1.call-done = bf16[64,2048]{1,0:T(8,128)(2,1)} async-done(((bf16[64,2048]{1,0:T(8,128)(2,1)}), bf16[64,2048]{1,0:T(8,128)(2,1)}) %all-reduce.2.cloned.1.call-update) | async-done | bytes 262160 | tf_op jit(solution)/shard_map/psum | solution.py:126
  62.9 1.1 multiply_reduce_fusion
  64.1 1.8 multiply_convert_fusion.1
  65.8 0.0 all-gather.6.cloned.1.call-update
  65.9 0.0 reduce-scatter.2.cloned.1.call-start
  65.9 32.7 %all_gather.33 = s32[16,64,8]{1,2,0:T(8,128)S(1)} all-gather(s32[1,64,8]{1,2,0:T(8,128)S(1)} %copy-done.5), channel_id=1, replica_groups=mesh['kv'=4,'seq'=4,'exp'=2] {'kv','seq'}, dimensions={0}, use_global_device_ids=true | all-gather | bytes 34816 | tf_op jit(solution)/shard_map/all_gather | solution.py:136
  98.6 0.2 compare_reduce_fusion
  98.8 0.9 reduce_window_sum.11
  99.8 17.3 %all-gather.6.cloned.1.call-done = bf16[1024,2048]{1,0:T(8,128)(2,1)} async-done(((bf16[64,2048]{1,0:T(8,128)(2,1)}), bf16[1024,2048]{1,0:T(8,128)(2,1)}) %all-gather.6.cloned.1.call-update) | async-done | bytes 4194320 | tf_op jit(solution)/shard_map/all_gather | solution.py:145
  117.1 3.6 %convert_bitcast_fusion = bf16[4,16,16,2048]{3,2,0,1:T(8,128)(2,1)S(1)} fusion(bf16[16,64,2048,1]{2,1,3,0:T(8,128)(2,1)} %bitcast.155, s32[16,4,64]{2,1,0:T(4,128)S(1)} %copy.60, pred[16,4,64]{2,1,0:T(4,128)(4,1)S(1)} %copy.59), kind=kOutput, calls=%fused_computation.3 | convolution fusion | flops 270663680 | bytes 8409088 | tf_op jit(solution)/shard_map/sect,std->escd/dot_general | solution.py:146
  120.7 0.0 slice-start.1
  120.7 0.3 copy.61
  121.0 0.0 copy-start.2
  121.0 1.2 fusion.31
  122.2 0.9 copy-done.2
  123.2 1.2 slice-done.1
  124.4 2.3 fusion.52
  126.7 13.7 %convolution_convert_fusion = bf16[4,256,2048]{2,1,0:T(8,128)(2,1)} fusion(bf16[4,512,2048]{2,1,0:T(8,128)(2,1)} %param.27, f32[4,256,512]{2,1,0:T(8,128)S(1)} %fusion.52, bf16[4,256,2048]{2,1,0:T(8,128)(2,1)} %bitcast.154, bf16[4,2048,512]{2,1,0:T(8,128)(2,1)} %param.26, f32[4,256]{1,0:T(4,128)S(1)} %fusion.42), kind=kOutput, calls=%fused_computation.4 | convolution fusion | flops 4300734464 | bytes 27267072 | tf_op jit(solution)/shard_map/erf,efd->erd/dot_general | solution.py:153
  140.4 3.5 %bitcast_convert_fusion = bf16[16,64,2048]{2,1,0:T(8,128)(2,1)S(1)} fusion(bf16[4,16,16,2048]{3,2,1,0:T(8,128)(2,1)} %bitcast.156, s32[16,4,64]{2,1,0:T(4,128)S(1)} %copy.60, pred[16,4,64]{2,1,0:T(4,128)(4,1)S(1)} %copy.59), kind=kOutput, calls=%fused_computation | convolution fusion | flops 270663680 | bytes 8409088 | tf_op jit(solution)/shard_map/sect,escd->std/dot_general | solution.py:156
  143.9 0.5 fusion.47
  144.4 0.0 copy-start.1
  144.4 2.5 pad_maximum_fusion
  146.9 0.0 reduce-scatter.2.cloned.1.call-update
  147.0 142.6 %reduce-scatter.2.cloned.1.call-done = bf16[1,64,1024]{2,1,0:T(8,128)(2,1)} async-done(((bf16[32,64,1024]{2,1,0:T(8,128)(2,1)}), bf16[1,64,1024]{2,1,0:T(8,128)(2,1)}) %reduce-scatter.2.cloned.1.call-update) | async-done | bytes 131088 | tf_op jit(solution)/shard_map/reduce_scatter | solution.py:159
  289.6 1.6 fusion.26
  291.2 0.0 copy-done.1
  (30 shorter events, 0.3 us)
Async XLA Ops:
  6.5 93.2 %copy-start = (bf16[2048,64]{0,1:T(8,128)(2,1)S(1)}, bf16[2048,64]{0,1:T(8,128)(2,1)}, u32[]{:S(2)}) copy-start(bf16[2048,64]{0,1:T(8,128)(2,1)} %param.23) | copy-start | bytes 786436
  6.5 56.4 %all-reduce.2.cloned.1.call-start = ((), (), s32[]{:S(2)}) async-start(), calls=%async_computation.1 | async-start | bytes 524288 | tf_op jit(solution)/shard_map/psum | solution.py:126
  16.4 21.4 %copy-start.4 = (bf16[2048]{0:T(1024)(128)(2,1)S(1)}, bf16[2048]{0:T(1024)(128)(2,1)}, u32[]{:S(2)}) copy-start(bf16[2048]{0:T(1024)(128)(2,1)} %param.21) | copy-start | bytes 12292
  16.5 46.5 %copy-start.3 = (bf16[1,64,2048]{2,1,0:T(8,128)(2,1)S(1)}, bf16[1,64,2048]{2,1,0:T(8,128)(2,1)}, u32[]{:S(2)}) copy-start(bf16[1,64,2048]{2,1,0:T(8,128)(2,1)} %param.20) | copy-start | bytes 786436
  33.6 32.4 %copy-start.5 = (s32[1,64,8]{1,2,0:T(8,128)S(1)}, s32[1,64,8]{1,2,0:T(8,128)}, u32[]{:S(2)}) copy-start(s32[1,64,8]{1,2,0:T(8,128)} %param.24) | copy-start | bytes 6148
  37.8 79.3 %all-gather.6.cloned.1.call-start = ((), (), s32[]{:S(2)}) async-start(), calls=%async_computation.3 | async-start | bytes 4456448 | tf_op jit(solution)/shard_map/all_gather | solution.py:145
  65.9 223.7 %reduce-scatter.2.cloned.1.call-start = ((), (), s32[]{:S(2)}) async-start(), calls=%async_computation.2 | async-start | bytes 4325376 | tf_op jit(solution)/shard_map/reduce_scatter | solution.py:159
  117.1 6.0 %slice-start = ((s8[8388608]{0:T(1024)(128)(4,1)}), s8[4194304]{0:T(1024)(128)(4,1)S(1)}, s32[]{:S(2)}) async-start(s8[8388608]{0:T(1024)(128)(4,1)} %bitcast.169), calls=%async_computation.4 | async-start | bytes 8388608
  120.7 3.7 %slice-start.1 = ((s8[8388608]{0:T(1024)(128)(4,1)}), s8[4194304]{0:T(1024)(128)(4,1)S(1)}, s32[]{:S(2)}) async-start(s8[8388608]{0:T(1024)(128)(4,1)} %bitcast.169), calls=%async_computation.5 | async-start | bytes 8388608
  121.0 2.1 copy-start.2
  144.4 146.8 %copy-start.1 = (bf16[2048,64]{0,1:T(8,128)(2,1)S(1)}, bf16[2048,64]{0,1:T(8,128)(2,1)}, u32[]{:S(2)}) copy-start(bf16[2048,64]{0,1:T(8,128)(2,1)} %param.23) | copy-start | bytes 786436
Sparse Core Ops, SparseCore 0:
  37.9 24.9 all-reduce.1
  66.0 51.0 all-gather.5
  147.1 142.4 reduce-scatter.1

commit v2 on v1

--- a/solution.py
+++ b/solution.py
@@ -1,6 +1,10 @@
+import functools
+
 import jax
 import jax.numpy as jnp
 from jax import lax
+from jax.experimental import pallas as pl
+from jax.experimental.pallas import tpu as pltpu
 from jax.sharding import PartitionSpec as P
 
 D = 2048
@@ -14,19 +18,181 @@
 EPS_NORM = 1e-06
 
 
-def merged(x, axis, combine):
-    everything = jax.tree.map(
-        lambda part, kind: lax.all_gather(part.astype(kind), axis),
-        x,
-        (jnp.bfloat16, jnp.bfloat16, jnp.bfloat16),
-    )
-
-    def take(k):
-        return jax.tree.map(lambda part, own: part[k].astype(own.dtype), everything, x)
-
-    return lax.fori_loop(
-        1, lax.axis_size(axis), lambda k, so_far: combine(so_far, take(k)), take(0)
-    )
+MESH = pl.DeviceIdType.MESH
+
+
+def bits_of(axis):
+    return [(axis, bit) for bit in range((lax.axis_size(axis) - 1).bit_length())]
+
+
+def my_bit(stage):
+    axis, bit = stage
+    return (lax.axis_index(axis) // 2**bit) % 2
+
+
+def partner(stage):
+    axis, bit = stage
+    return {axis: lax.axis_index(axis) + (1 - 2 * my_bit(stage)) * 2**bit}
+
+
+def greet(stages):
+    barrier = pltpu.get_barrier_semaphore()
+    for stage in stages:
+        pl.semaphore_signal(barrier, inc=1, device_id=partner(stage), device_id_type=MESH)
+    pl.semaphore_wait(barrier, len(stages))
+
+
+def gather_kernel(orders, *refs):
+    count = len(orders)
+    ins, outs = refs[:count], refs[count : 2 * count]
+    send_sem, recv_sem = refs[2 * count :]
+    for i, order in enumerate(orders):
+        place = sum(my_bit(stage) * 2**k for k, stage in enumerate(order))
+        outs[i][place] = ins[i][...]
+    greet(sorted(orders[0]))
+    copies = [[] for order in orders]
+    for k in range(len(orders[0])):
+        for i, order in enumerate(orders):
+            if k > 0:
+                copies[i][k - 1].wait_recv()
+            base = sum(my_bit(stage) * 2**j for j, stage in enumerate(order) if j >= k)
+            region = outs[i].at[pl.ds(base, 2**k)]
+            copy = pltpu.make_async_remote_copy(
+                src_ref=region,
+                dst_ref=region,
+                send_sem=send_sem.at[i, k],
+                recv_sem=recv_sem.at[i, k],
+                device_id=partner(order[k]),
+                device_id_type=MESH,
+            )
+            copy.start()
+            copies[i].append(copy)
+    for i in range(count):
+        copies[i][-1].wait_recv()
+    for i in range(count):
+        for copy in copies[i]:
+            copy.wait_send()
+
+
+def gather_all(parts, orders, ident):
+    steps = len(orders[0])
+    vmem = pl.BlockSpec(memory_space=pltpu.VMEM)
+    return pl.pallas_call(
+        functools.partial(gather_kernel, orders),
+        out_shape=[jax.ShapeDtypeStruct((2**steps,) + part.shape, part.dtype) for part in parts],
+        in_specs=[vmem] * len(parts),
+        out_specs=[vmem] * len(parts),
+        scratch_shapes=[
+            pltpu.SemaphoreType.DMA((len(parts), steps)),
+            pltpu.SemaphoreType.DMA((len(parts), steps)),
+        ],
+        compiler_params=pltpu.CompilerParams(
+            collective_id=ident, has_side_effects=True, vmem_limit_bytes=56 * 2**20
+        ),
+    )(*parts)
+
+
+def reduce_kernel(orders, *refs):
+    count, steps = len(orders), len(orders[0])
+    ins, outs = refs[:count], refs[count : 2 * count]
+    buffers = refs[2 * count : 2 * count + count * steps]
+    send_sem, recv_sem = refs[2 * count + count * steps :]
+    greet(sorted(orders[0]))
+    copies = [[] for order in orders]
+
+    def held(i, k):
+        return ins[i] if k == 0 else buffers[i * steps + k - 1]
+
+    def add_in(i, k):
+        half = 2 ** (steps - 1 - k)
+        base = my_bit(orders[i][k]) * half
+        mine, came = held(i, k), buffers[i * steps + k]
+
+        def one(j, carry):
+            total = mine[base + j].astype(jnp.float32) + came[j].astype(jnp.float32)
+            if k == steps - 1:
+                outs[i][...] = total
+            else:
+                came[j] = total.astype(came.dtype)
+            return carry
+
+        lax.fori_loop(0, half, one, 0)
+
+    for k in range(steps):
+        half = 2 ** (steps - 1 - k)
+        for i, order in enumerate(orders):
+            if k > 0:
+                copies[i][k - 1].wait_recv()
+                add_in(i, k - 1)
+            copy = pltpu.make_async_remote_copy(
+                src_ref=held(i, k).at[pl.ds((1 - my_bit(order[k])) * half, half)],
+                dst_ref=buffers[i * steps + k],
+                send_sem=send_sem.at[i, k],
+                recv_sem=recv_sem.at[i, k],
+                device_id=partner(order[k]),
+                device_id_type=MESH,
+            )
+            copy.start()
+            copies[i].append(copy)
+    for i in range(count):
+        copies[i][-1].wait_recv()
+        add_in(i, steps - 1)
+    for i in range(count):
+        for copy in copies[i]:
+            copy.wait_send()
+
+
+def reduce_all(parts, orders, ident):
+    steps = len(orders[0])
+    vmem = pl.BlockSpec(memory_space=pltpu.VMEM)
+    return pl.pallas_call(
+        functools.partial(reduce_kernel, orders),
+        out_shape=[jax.ShapeDtypeStruct(part.shape[1:], jnp.float32) for part in parts],
+        in_specs=[vmem] * len(parts),
+        out_specs=[vmem] * len(parts),
+        scratch_shapes=[
+            pltpu.VMEM((2 ** (steps - 1 - k),) + part.shape[1:], part.dtype)
+            for part in parts
+            for k in range(steps)
+        ]
+        + [
+            pltpu.SemaphoreType.DMA((len(parts), steps)),
+            pltpu.SemaphoreType.DMA((len(parts), steps)),
+        ],
+        compiler_params=pltpu.CompilerParams(
+            collective_id=ident, has_side_effects=True, vmem_limit_bytes=56 * 2**20
+        ),
+    )(*parts)
+
+
+def bit_axes():
+    return [stage for axis in ("kv", "seq", "exp") for stage in bits_of(axis)[::-1]]
+
+
+def spread_bits(x, order):
+    names = bit_axes()
+    x = x.reshape((2,) * len(names) + x.shape[1:])
+    tail = range(len(names), x.ndim)
+    x = jnp.transpose(x, [names.index(stage) for stage in order] + list(tail))
+    return x.reshape((2 ** len(names),) + x.shape[len(names) :])
+
+
+def collect_bits(x, order):
+    names = bit_axes()
+    x = x.reshape((2,) * len(names) + x.shape[1:])
+    tail = range(len(names), x.ndim)
+    x = jnp.transpose(x, [order.index(stage) for stage in names] + list(tail))
+    return x.reshape((2 ** len(names),) + x.shape[len(names) :])
+
+
+def stream_orders(count):
+    kv, seq, exp = bits_of("kv"), bits_of("seq"), bits_of("exp")
+    orders = (kv + exp + seq[::-1], kv[:1] + exp + kv[1:] + seq[::-1])
+    return [orders[i % 2] for i in range(count)]
+
+
+def columns_cut(x, width):
+    return [x[..., k : k + width] for k in range(0, x.shape[-1], width)]
 
 
 def ancestry(parents, draft_len):
@@ -117,24 +283,69 @@
     )
     row_max = jnp.transpose(row_max, (0, 2, 1))
     row_sum = jnp.transpose(row_sum, (0, 2, 1))
-    row_max, row_sum, weighted = merged((row_max, row_sum, weighted), "exp", merge_pair)
+    token_rows = req_count * draft_len
+    column_count = D // set_count
+    exp_bits = bits_of("exp")
+    stats = jnp.concatenate([row_max, row_sum], axis=2).reshape(token_rows, 2 * H)
+    stats = jnp.pad(stats, ((0, 0), (0, 128 - 2 * H)))
+    all_weighted, all_stats = gather_all(
+        [weighted.astype(jnp.bfloat16).reshape(token_rows, D), stats], [exp_bits, exp_bits], 1
+    )
+
+    def one_set(k):
+        return (
+            all_stats[k, :, :H].reshape(row_max.shape),
+            all_stats[k, :, H : 2 * H].reshape(row_sum.shape),
+            all_weighted[k].astype(jnp.float32).reshape(weighted.shape),
+        )
+
+    row_max, row_sum, weighted = functools.reduce(
+        merge_pair, [one_set(k) for k in range(set_count)]
+    )
     attended = (weighted / row_sum[..., None]).astype(jnp.bfloat16)
     attended = lax.dynamic_slice_in_dim(attended, my_set * head_share, head_share, 2)
-    token_rows = req_count * draft_len
     attended = attended.reshape(token_rows, head_share * head_dim)
     partial_value = jnp.dot(attended, out_proj, preferred_element_type=jnp.float32)
-    projected = lax.psum(partial_value.astype(jnp.bfloat16), "exp").astype(jnp.float32)
-    residual = hidden.reshape(token_rows, D).astype(jnp.float32) + projected
-    mean_sq = jnp.mean(residual * residual, axis=1, keepdims=True)
+    by_columns = jnp.transpose(
+        partial_value.astype(jnp.bfloat16).reshape(token_rows, set_count, column_count), (1, 0, 2)
+    )
+    (projected,) = reduce_all([by_columns], [exp_bits[::-1]], 2)
+
+    def own_part(x):
+        return lax.dynamic_slice_in_dim(x, my_set * column_count, column_count, x.ndim - 1)
+
+    residual = own_part(hidden.reshape(token_rows, D)).astype(jnp.float32) + projected
+    own_sq = jnp.sum(residual * residual, axis=1, keepdims=True)
+    (all_sq,) = gather_all([jnp.broadcast_to(own_sq, (token_rows, 128))], [exp_bits], 3)
+    mean_sq = jnp.sum(all_sq[:, :, :1], axis=0) / D
     normed = (
-        residual * lax.rsqrt(mean_sq + EPS_NORM) * norm_gain.astype(jnp.float32)[None, :]
+        residual * lax.rsqrt(mean_sq + EPS_NORM) * own_part(norm_gain).astype(jnp.float32)[None, :]
     ).astype(jnp.bfloat16)
-    spread = ("kv", "seq")
+    width = max(128, column_count // 4)
+    streams = column_count // width
+    orders = stream_orders(streams)
     local_experts = gate_w.shape[0]
-    column_count = D // set_count
     my_block = lax.axis_index("kv") * lax.axis_size("seq") + lax.axis_index("seq")
-    all_routes = lax.all_gather(routes.reshape(token_rows, TOPK), spread)
-    sources = all_routes.shape[0]
+    routes_row = jnp.pad(
+        jnp.transpose(routes.reshape(token_rows, TOPK)), ((0, 0), (0, -token_rows % 128))
+    )
+    gathered = gather_all(
+        columns_cut(normed, width) + [routes_row],
+        [order[::-1] for order in orders] + [orders[0][::-1]],
+        4,
+    )
+    sources = lax.axis_size("kv") * lax.axis_size("seq")
+    all_routes = collect_bits(gathered[-1], orders[0]).reshape(
+        (sources, set_count) + routes_row.shape
+    )[:, 0, :, :token_rows]
+    all_routes = jnp.transpose(all_routes, (0, 2, 1))
+    by_stream = [
+        collect_bits(part, order).reshape(sources, set_count, token_rows, width)
+        for part, order in zip(gathered, orders)
+    ]
+    all_rows = jnp.transpose(jnp.stack(by_stream, axis=3), (0, 2, 1, 3, 4)).reshape(
+        sources, token_rows, D
+    )
     expert_ids = my_block * local_experts + jnp.arange(local_experts, dtype=jnp.int32)
     member = jnp.any(all_routes[:, None] == expert_ids[None, :, None, None], axis=3).astype(jnp.int32)
     rank = jnp.cumsum(member, axis=2) - member
@@ -142,7 +353,6 @@
         rank[:, :, None, :] == jnp.arange(CAP, dtype=jnp.int32)[None, None, :, None]
     )
     chosen = chosen.astype(jnp.bfloat16)
-    all_rows = lax.all_gather(normed, spread)
     picked = jnp.einsum("sect,std->escd", chosen, all_rows, preferred_element_type=jnp.float32)
     picked = picked.astype(jnp.bfloat16).reshape(local_experts, sources * CAP, D)
     own_router = lax.dynamic_slice_in_dim(router, my_block * local_experts, local_experts, 1)
@@ -156,12 +366,16 @@
     combined = jnp.einsum("sect,escd->std", chosen, finished, preferred_element_type=jnp.float32)
     combined = combined.astype(jnp.bfloat16).reshape(sources, token_rows, set_count, column_count)
     combined = jnp.transpose(combined, (0, 2, 1, 3)).reshape(-1, token_rows, column_count)
-    summed_share = lax.psum_scatter(
-        combined, ("kv", "seq", "exp"), scatter_dimension=0, tiled=True
-    )[0].astype(jnp.float32)
-    own_columns = lax.dynamic_slice_in_dim(residual, my_set * column_count, column_count, 1)
+    summed_share = jnp.concatenate(
+        reduce_all(
+            [spread_bits(part, order) for part, order in zip(columns_cut(combined, width), orders)],
+            orders,
+            5,
+        ),
+        axis=1,
+    )
     return (
-        (own_columns + summed_share)
+        (residual + summed_share)
         .astype(jnp.bfloat16)
         .reshape(req_count, draft_len, column_count)
     )

time: 298 us -> 179 us (0.60)
  waiting for transfers between devices: 185 us -> 0 us
  Pallas kernels: 0 us -> 101 us
  blocking collectives: 49.3 us -> 0 us
  local copies, waits for them, and re-layouts: 8.27 us -> 35.1 us
  between operations: 14.2 us -> 1.21 us
  matrix products: 30.2 us -> 27.2 us
    reduce_scatter x1 -> x0, waiting for transfers between devices: 143 us -> none  [local(): lax.psum_scatter(combined, ('kv', 'seq', 'exp'), scatter_dimension=0, til...]
    pallas_call x0 -> x5, Pallas kernels: none -> 101 us  [the longest x3 58 us: gather_all(): pl.pallas_call(functools.partial(gather_kernel, orders), out_shape=[jax.S...]
    all_gather x4 -> x0, blocking collectives: 49.3 us -> none  [the longest x1 32.7 us: local(): all_routes = lax.all_gather(routes.reshape(token_rows, TOPK), spread)]
    psum x1 -> x0, waiting for transfers between devices: 25.1 us -> none  [local(): lax.psum(partial_value.astype(jnp.bfloat16), 'exp').astype(jnp.float32)]
    all_gather x1 -> x0, waiting for transfers between devices: 17.3 us -> none  [local(): all_rows = lax.all_gather(normed, spread)]
    reshape x0 -> x7, local copies, waits for them, and re-layouts: none -> 12.3 us  [the longest x1 7.77 us: local(): jnp.transpose(jnp.stack(by_stream, axis=3), (0, 2, 1, 3, 4))]
    transpose x0 -> x6, local copies, waits for them, and re-layouts: none -> 9.83 us  [the longest x1 5.4 us: local(): jnp.transpose(jnp.stack(by_stream, axis=3), (0, 2, 1, 3, 4))]
  transfers between devices with their start and end apart: 3 -> 0, of which waited for: 3 -> 0; matrix products, arithmetic and copies ran while one was open for 0% -> 0% of each run, Pallas kernels for 0% -> 0%
where the time goes in v2:
time: 179 us; the launch traced here: 177 us
  Pallas kernels  101 us (56%)
  local copies, waits for them, and re-layouts  35.1 us (20%)
  matrix products  27.2 us (15%)
  other arithmetic  12.3 us (7%)
    pallas_call x3, Pallas kernels, gather_all(): pl.pallas_call(functools.partial(gather_kernel, orders), out_shape=[jax.S...  58 us
    pallas_call x2, Pallas kernels, reduce_all(): pl.pallas_call(functools.partial(reduce_kernel, orders), out_shape=[jax.S...  43.4 us
    dot_general x1, matrix products, local(): jnp.einsum('erf,efd->erd', activity.astype(jnp.bfloat16), down_w, preferr...  13.6 us
    reshape x1, local copies, waits for them, and re-layouts, local(): jnp.transpose(jnp.stack(by_stream, axis=3), (0, 2, 1, 3, 4))  7.77 us
    unnamed x31, local copies, waits for them, and re-layouts  5.49 us
    transpose x1, local copies, waits for them, and re-layouts, local(): jnp.transpose(jnp.stack(by_stream, axis=3), (0, 2, 1, 3, 4))  5.4 us
    transpose x4, local copies, waits for them, and re-layouts, spread_bits(): x = jnp.transpose(x, [names.index(stage) for stage in order] + list(tail))  4.42 us
    reshape x5, local copies, waits for them, and re-layouts, collect_bits(): x = x.reshape((2,) * len(names) + x.shape[1:])  3.85 us

profile of v2, /device:TPU:0, one launch (start us, length us, event | category | flops | bytes accessed | tf_op | source)
XLA Modules:
  0.0 177.3 jit_solution(12885625483595612594)
XLA Ops:
  0.7 0.7 fusion.44
  1.5 0.7 dynamic-slice_convert_fusion
  2.2 1.3 pad.9.refs_4_
  3.8 0.8 fusion.35
  4.6 0.2 convolution_minimum_fusion.4
  4.7 0.2 convolution_minimum_fusion.3
  4.9 0.2 convolution_minimum_fusion.2
  5.1 0.2 convolution_minimum_fusion.1
  5.2 0.2 convolution_minimum_fusion
  5.4 0.2 fusion.57
  5.7 1.0 copy.105
  6.7 1.0 slice_bitcast_fusion
  7.9 1.5 fusion.54
  9.4 0.2 copy.103
  9.6 0.2 copy.75
  9.8 0.8 fusion.56
  10.6 0.2 copy.106
  10.7 0.2 copy.72
  11.0 0.5 fusion.7
  11.5 0.4 fusion.12
  11.9 0.2 copy.78
  12.1 0.8 copy.132
  13.1 0.6 pad.8.refs_1_
  13.7 12.2 %shard_map.139 = (bf16[2,64,2048]{2,1,0:T(8,128)(2,1)}, f32[2,64,128]{2,1,0:T(8,128)}) custom-call(bf16[64,2048]{1,0:T(8,128)(2,1)} %bitcast.217, f32[64,128]{1,0:T(8,128)} %pad.8.refs_1_), custom_call_target="tpu_custom_call" | custom-call | tf_op jit(solution)/shard_map/pallas_call | solution.py:80
  25.9 0.9 fusion.43
  27.0 1.1 convert_bitcast_fusion.2
  28.4 0.3 fusion.27
  28.7 0.8 convolution_convert_fusion.1
  29.5 0.7 copy.133
  30.2 6.7 %shard_map.140 = f32[64,1024]{1,0:T(8,128)} custom-call(bf16[2,64,1024]{2,1,0:T(8,128)(2,1)} %bitcast.219), custom_call_target="tpu_custom_call" | custom-call | tf_op jit(solution)/shard_map/pallas_call | solution.py:148
  36.9 1.1 multiply_reduce_fusion
  38.0 0.7 broadcast_in_dim.43.refs_0_
  38.7 5.3 %shard_map.141 = f32[2,64,128]{2,1,0:T(8,128)} custom-call(f32[64,128]{1,0:T(8,128)} %broadcast_in_dim.43.refs_0_), custom_call_target="tpu_custom_call" | custom-call | tf_op jit(solution)/shard_map/pallas_call | solution.py:80
  44.0 0.9 slice_reduce_fusion
  45.0 1.1 multiply_convert_fusion.1
  46.1 0.6 fusion.55
  46.7 40.6 %shard_map.142 = (bf16[32,64,256]{2,1,0:T(8,128)(2,1)}, bf16[32,64,256]{2,1,0:T(8,128)(2,1)}, bf16[32,64,256]{2,1,0:T(8,128)(2,1)}, bf16[32,64,256]{2,1,0:T(8,128)(2,1)}, s32[32,8,128]{2,1,0:T(8,128)}) custom-call(bf16[64,256]{1,0:T(8,128)(2,1)} %get-tuple-element.42.refs_0_, bf16[64,256]{1,0:T(8,128)(2,1)} %get-tuple-element.41.refs_1_, ...), custom_call_target="tpu_custom_call" | custom-call | tf_op jit(solution)/shard_map/pallas_call | solution.py:80
  87.3 1.1 copy.82
  88.4 0.2 compare_reduce_fusion
  88.5 1.3 copy.86
  89.9 0.9 reduce_window_sum.11
  90.8 1.3 copy.87
  92.1 0.1 copy.88
  92.2 0.1 copy.89
  92.3 0.6 maximum_bitcast_fusion
  92.9 5.4 %copy.90 = bf16[16,64,2,4,256]{4,3,2,1,0:T(4,128)(2,1)} copy(bf16[16,64,2,4,256]{4,1,2,0,3:T(8,128)(2,1)S(1)} %maximum_bitcast_fusion) | data formatting | bytes 8388608 | tf_op jit(solution)/shard_map/transpose | solution.py:346
  98.3 7.8 %reshape.487 = bf16[16,64,2048,1]{2,1,0,3:T(8,128)(2,1)} reshape(bf16[16,64,2,4,256]{4,3,2,1,0:T(4,128)(2,1)} %copy.90) | data formatting | bytes 8388608 | tf_op jit(solution)/shard_map/reshape | solution.py:346
  106.1 3.6 %convert_bitcast_fusion = bf16[4,16,16,2048]{3,2,0,1:T(8,128)(2,1)S(1)} fusion(bf16[16,64,2048,1]{2,1,0,3:T(8,128)(2,1)} %reshape.487, s32[16,4,64]{2,1,0:T(4,128)S(1)} %copy.85, pred[16,4,64]{2,1,0:T(4,128)(4,1)S(1)} %copy.84), kind=kOutput, calls=%fused_computation.6 | convolution fusion | flops 270663680 | bytes 8409088 | tf_op jit(solution)/shard_map/sect,std->escd/dot_general | solution.py:356
  109.7 0.3 copy.91
  110.0 1.2 fusion.37
  111.2 0.9 copy-done.2
  112.1 1.2 slice-done.1
  113.4 2.3 %fusion.58 = f32[4,256,512]{2,1,0:T(8,128)S(1)} fusion(bf16[4,256,2048]{2,1,0:T(8,128)(2,1)S(1)} %bitcast.190, bf16[4,2048,512]{2,1,0:T(8,128)(2,1)S(1)} %bitcast.233), kind=kOutput, calls=%fused_computation.107 | convolution fusion | flops 2147483648 | bytes 14680064 | tf_op jit(solution)/shard_map/erd,edf->erf/dot_general | solution.py:360
  115.7 13.6 %convolution_convert_fusion = bf16[4,256,2048]{2,1,0:T(8,128)(2,1)} fusion(bf16[4,512,2048]{2,1,0:T(8,128)(2,1)} %param.27, f32[4,256,512]{2,1,0:T(8,128)S(1)} %fusion.58, bf16[4,256,2048]{2,1,0:T(8,128)(2,1)} %bitcast.191, bf16[4,2048,512]{2,1,0:T(8,128)(2,1)} %param.26, f32[4,256]{1,0:T(4,128)S(1)} %fusion.47), kind=kOutput, calls=%fused_computation.7 | convolution fusion | flops 4300734464 | bytes 27267072 | tf_op jit(solution)/shard_map/erf,efd->erd/dot_general | solution.py:363
  129.3 3.5 %bitcast_convert_fusion = bf16[16,64,2048]{2,1,0:T(8,128)(2,1)S(1)} fusion(bf16[4,16,16,2048]{3,2,1,0:T(8,128)(2,1)} %bitcast.193, s32[16,4,64]{2,1,0:T(4,128)S(1)} %copy.85, pred[16,4,64]{2,1,0:T(4,128)(4,1)S(1)} %copy.84), kind=kOutput, calls=%fused_computation | convolution fusion | flops 270663680 | bytes 8409088 | tf_op jit(solution)/shard_map/sect,escd->std/dot_general | solution.py:366
  132.8 0.5 fusion.53
  133.3 0.6 pad_maximum_fusion
  133.9 0.6 fusion.52
  134.5 1.1 copy.96
  135.6 1.1 copy.95
  136.7 1.1 copy.94
  137.8 1.1 copy.93
  138.9 36.7 %shard_map.143 = (f32[64,256]{1,0:T(8,128)}, f32[64,256]{1,0:T(8,128)}, f32[64,256]{1,0:T(8,128)}, f32[64,256]{1,0:T(8,128)}) custom-call(bf16[32,64,256]{2,1,0:T(8,128)(2,1)} %bitcast.197, bf16[32,64,256]{2,1,0:T(8,128)(2,1)} %bitcast.196, bf16[32,64,256]{2,1,0:T(8,128)(2,1)} %bitcast.195, bf16[32,64,256]{2,1,0:T(8,128)(2,1)} %bitcast.194), custom_call_target="tpu_custom_call" | custom-call | tf_op jit(solution)/shard_map/pallas_call | solution.py:148
  175.6 1.6 fusion.30
  (50 shorter events, 1.3 us)
Async XLA Ops:
  0.0 3.7 %copy-start = (bf16[2048,64]{0,1:T(8,128)(2,1)S(1)}, bf16[2048,64]{0,1:T(8,128)(2,1)}, u32[]{:S(2)}) copy-start(bf16[2048,64]{0,1:T(8,128)(2,1)} %param.23) | copy-start | bytes 786436
  13.0 15.7 %copy-start.3 = (bf16[1024,2048]{1,0:T(8,128)(2,1)S(1)}, bf16[1024,2048]{1,0:T(8,128)(2,1)}, u32[]{:S(2)}) copy-start(bf16[1024,2048]{1,0:T(8,128)(2,1)} %param.22) | copy-start | bytes 12582916
  28.2 8.8 %copy-start.7 = (bf16[1,64,2048]{2,1,0:T(8,128)(2,1)S(1)}, bf16[1,64,2048]{2,1,0:T(8,128)(2,1)}, u32[]{:S(2)}) copy-start(bf16[1,64,2048]{2,1,0:T(8,128)(2,1)} %param.20) | copy-start | bytes 786436
  87.3 4.8 %copy-start.6 = (bf16[32,64,256]{2,1,0:T(8,128)(2,1)S(1)}, bf16[32,64,256]{2,1,0:T(8,128)(2,1)}, u32[]{:S(2)}) copy-start(bf16[32,64,256]{2,1,0:T(8,128)(2,1)} %get-tuple-element.21) | copy-start | bytes 3145732
  87.3 4.9 %copy-start.5 = (bf16[32,64,256]{2,1,0:T(8,128)(2,1)S(1)}, bf16[32,64,256]{2,1,0:T(8,128)(2,1)}, u32[]{:S(2)}) copy-start(bf16[32,64,256]{2,1,0:T(8,128)(2,1)} %get-tuple-element.22) | copy-start | bytes 3145732
  106.1 6.0 %slice-start = ((s8[8388608]{0:T(1024)(128)(4,1)}), s8[4194304]{0:T(1024)(128)(4,1)S(1)}, s32[]{:S(2)}) async-start(s8[8388608]{0:T(1024)(128)(4,1)} %bitcast.232), calls=%async_computation | async-start | bytes 8388608
  109.7 3.7 %slice-start.1 = ((s8[8388608]{0:T(1024)(128)(4,1)}), s8[4194304]{0:T(1024)(128)(4,1)S(1)}, s32[]{:S(2)}) async-start(s8[8388608]{0:T(1024)(128)(4,1)} %bitcast.232), calls=%async_computation.1 | async-start | bytes 8388608
  110.0 2.1 %copy-start.2 = (bf16[4,16,16,2048]{3,2,1,0:T(8,128)(2,1)}, bf16[4,16,16,2048]{3,2,1,0:T(8,128)(2,1)S(1)}, u32[]{:S(2)}) copy-start(bf16[4,16,16,2048]{3,2,1,0:T(8,128)(2,1)S(1)} %copy.91) | copy-start | bytes 12582916
  136.7 40.6 %copy-start.1 = (bf16[2048,64]{0,1:T(8,128)(2,1)S(1)}, bf16[2048,64]{0,1:T(8,128)(2,1)}, u32[]{:S(2)}) copy-start(bf16[2048,64]{0,1:T(8,128)(2,1)} %param.23) | copy-start | bytes 786436
  136.7 38.9 %copy-start.4 = (f32[64,1024]{1,0:T(8,128)S(1)}, f32[64,1024]{1,0:T(8,128)}, u32[]{:S(2)}) copy-start(f32[64,1024]{1,0:T(8,128)} %shard_map.140) | copy-start | bytes 786436
  136.7 38.9 %copy-start.8 = (bf16[1,64,2048]{2,1,0:T(8,128)(2,1)S(1)}, bf16[1,64,2048]{2,1,0:T(8,128)(2,1)}, u32[]{:S(2)}) copy-start(bf16[1,64,2048]{2,1,0:T(8,128)(2,1)} %param.20) | copy-start | bytes 786436

commit v3 on v2

--- a/solution.py
+++ b/solution.py
@@ -35,6 +35,12 @@
     return {axis: lax.axis_index(axis) + (1 - 2 * my_bit(stage)) * 2**bit}
 
 
+def starts_of(parts, steps):
+    if steps < 3:
+        return [0] * len(parts)
+    return [2 if i // 2 % 2 == 1 else 0 for i in range(len(parts))]
+
+
 def greet(stages):
     barrier = pltpu.get_barrier_semaphore()
     for stage in stages:
@@ -42,7 +48,7 @@
     pl.semaphore_wait(barrier, len(stages))
 
 
-def gather_kernel(orders, *refs):
+def gather_kernel(orders, starts, *refs):
     count = len(orders)
     ins, outs = refs[:count], refs[count : 2 * count]
     send_sem, recv_sem = refs[2 * count :]
@@ -51,10 +57,15 @@
         outs[i][place] = ins[i][...]
     greet(sorted(orders[0]))
     copies = [[] for order in orders]
-    for k in range(len(orders[0])):
+    for slot in range(len(orders[0]) + max(starts)):
         for i, order in enumerate(orders):
+            k = slot - starts[i]
+            if k < 0 or k > len(order):
+                continue
             if k > 0:
                 copies[i][k - 1].wait_recv()
+            if k == len(order):
+                continue
             base = sum(my_bit(stage) * 2**j for j, stage in enumerate(order) if j >= k)
             region = outs[i].at[pl.ds(base, 2**k)]
             copy = pltpu.make_async_remote_copy(
@@ -67,8 +78,9 @@
             )
             copy.start()
             copies[i].append(copy)
-    for i in range(count):
-        copies[i][-1].wait_recv()
+    for i, order in enumerate(orders):
+        if starts[i] == max(starts):
+            copies[i][-1].wait_recv()
     for i in range(count):
         for copy in copies[i]:
             copy.wait_send()
@@ -78,7 +90,7 @@
     steps = len(orders[0])
     vmem = pl.BlockSpec(memory_space=pltpu.VMEM)
     return pl.pallas_call(
-        functools.partial(gather_kernel, orders),
+        functools.partial(gather_kernel, orders, starts_of(parts, steps)),
         out_shape=[jax.ShapeDtypeStruct((2**steps,) + part.shape, part.dtype) for part in parts],
         in_specs=[vmem] * len(parts),
         out_specs=[vmem] * len(parts),
@@ -92,7 +104,7 @@
     )(*parts)
 
 
-def reduce_kernel(orders, *refs):
+def reduce_kernel(orders, starts, *refs):
     count, steps = len(orders), len(orders[0])
     ins, outs = refs[:count], refs[count : 2 * count]
     buffers = refs[2 * count : 2 * count + count * steps]
@@ -118,12 +130,17 @@
 
         lax.fori_loop(0, half, one, 0)
 
-    for k in range(steps):
-        half = 2 ** (steps - 1 - k)
+    for slot in range(steps + max(starts)):
         for i, order in enumerate(orders):
+            k = slot - starts[i]
+            if k < 0 or k > steps:
+                continue
             if k > 0:
                 copies[i][k - 1].wait_recv()
                 add_in(i, k - 1)
+            if k == steps:
+                continue
+            half = 2 ** (steps - 1 - k)
             copy = pltpu.make_async_remote_copy(
                 src_ref=held(i, k).at[pl.ds((1 - my_bit(order[k])) * half, half)],
                 dst_ref=buffers[i * steps + k],
@@ -135,8 +152,9 @@
             copy.start()
             copies[i].append(copy)
     for i in range(count):
-        copies[i][-1].wait_recv()
-        add_in(i, steps - 1)
+        if starts[i] == max(starts):
+            copies[i][-1].wait_recv()
+            add_in(i, steps - 1)
     for i in range(count):
         for copy in copies[i]:
             copy.wait_send()
@@ -146,7 +164,7 @@
     steps = len(orders[0])
     vmem = pl.BlockSpec(memory_space=pltpu.VMEM)
     return pl.pallas_call(
-        functools.partial(reduce_kernel, orders),
+        functools.partial(reduce_kernel, orders, starts_of(parts, steps)),
         out_shape=[jax.ShapeDtypeStruct(part.shape[1:], jnp.float32) for part in parts],
         in_specs=[vmem] * len(parts),
         out_specs=[vmem] * len(parts),
@@ -165,16 +183,108 @@
     )(*parts)
 
 
+def expert_kernel(orders, counts, select_ref, back_ref, router_ref, *refs):
+    sources, sets, seq_count = counts
+    streams, steps = len(orders), len(orders[0])
+    ins = refs[:streams]
+    weights_in = refs[streams : streams + 3]
+    outs = refs[streams + 3 : 2 * streams + 3]
+    weights = refs[2 * streams + 3 : 2 * streams + 6]
+    rows_in, rows_out, sem = refs[2 * streams + 6 :]
+    experts = weights[0].shape[0]
+    width = ins[0].shape[2]
+    places = 2**steps
+
+    def copy_of(j, e):
+        return pltpu.make_async_copy(weights_in[j].at[e], weights[j].at[e], sem.at[j, e])
+
+    for e in range(experts):
+        for j in range(3):
+            copy_of(j, e).start()
+
+    def whose(order, p):
+        source, column_set = 0, 0
+        for k, (axis, bit) in enumerate(order):
+            value = (p // 2 ** (steps - 1 - k)) % 2
+            if axis == "exp":
+                column_set = column_set + value * 2**bit
+            else:
+                source = source + value * 2**bit * (seq_count if axis == "kv" else 1)
+        return source, column_set
+
+    def pick(p, carry):
+        for i, order in enumerate(orders):
+            source, column_set = whose(order, p)
+            rows = jnp.dot(select_ref[source], ins[i][p], preferred_element_type=jnp.float32)
+            rows = rows.astype(jnp.bfloat16)
+            for e in range(experts):
+                rows_in[
+                    column_set * streams + i, e, pl.ds(pl.multiple_of(source * CAP, CAP), CAP), :
+                ] = rows[e * CAP : (e + 1) * CAP]
+        return carry
+
+    lax.fori_loop(0, places, pick, 0)
+    blocks = sets * streams
+    for e in range(experts):
+        for j in range(3):
+            copy_of(j, e).wait()
+        gate_pre = up_pre = logits = 0.0
+        for k in range(blocks):
+            cut = slice(k * width, (k + 1) * width)
+            rows = rows_in[k, e]
+            gate_pre += jnp.dot(rows, weights[0][e, cut, :], preferred_element_type=jnp.float32)
+            up_pre += jnp.dot(rows, weights[1][e, cut, :], preferred_element_type=jnp.float32)
+            logits += jnp.dot(rows, router_ref[cut, :], preferred_element_type=jnp.float32)
+        activity = jax.nn.silu(gate_pre) * up_pre * jax.nn.sigmoid(logits[:, e : e + 1])
+        activity = activity.astype(jnp.bfloat16)
+        for k in range(blocks):
+            cut = slice(k * width, (k + 1) * width)
+            part = jnp.dot(activity, weights[2][e, :, cut], preferred_element_type=jnp.float32)
+            rows_out[k, :, e * CAP : (e + 1) * CAP, :] = part.astype(jnp.bfloat16).reshape(
+                sources, CAP, width
+            )
+
+    def combine(p, carry):
+        for i, order in enumerate(orders):
+            source, column_set = whose(order, p)
+            outs[i][p] = jnp.dot(
+                back_ref[source],
+                rows_out[column_set * streams + i, source],
+                preferred_element_type=jnp.float32,
+            ).astype(jnp.bfloat16)
+        return carry
+
+    lax.fori_loop(0, places, combine, 0)
+
+
+def expert_sums(parts, orders, chosen, router, weights):
+    sources, experts, _, tokens = chosen.shape
+    sets = lax.axis_size("exp")
+    width = parts[0].shape[2]
+    select = chosen.reshape(sources, experts * CAP, tokens)
+    vmem = pl.BlockSpec(memory_space=pltpu.VMEM)
+    blocks = sets * len(parts)
+    flops = 6 * experts * sources * CAP * weights[0].shape[1] * weights[0].shape[2]
+    return pl.pallas_call(
+        functools.partial(expert_kernel, orders, (sources, sets, lax.axis_size("seq"))),
+        out_shape=[jax.ShapeDtypeStruct(part.shape, part.dtype) for part in parts],
+        in_specs=[vmem] * (3 + len(parts)) + [pl.BlockSpec(memory_space=pl.ANY)] * 3,
+        out_specs=[vmem] * len(parts),
+        scratch_shapes=[pltpu.VMEM(weight.shape, weight.dtype) for weight in weights]
+        + [
+            pltpu.VMEM((blocks, experts, sources * CAP, width), jnp.bfloat16),
+            pltpu.VMEM((blocks, sources, experts * CAP, width), jnp.bfloat16),
+            pltpu.SemaphoreType.DMA((3, experts)),
+        ],
+        compiler_params=pltpu.CompilerParams(vmem_limit_bytes=58 * 2**20),
+        cost_estimate=pl.CostEstimate(
+            flops=flops, bytes_accessed=3 * weights[0].size * 2, transcendentals=0
+        ),
+    )(select, jnp.swapaxes(select, 1, 2), router, *parts, *weights)
+
+
 def bit_axes():
     return [stage for axis in ("kv", "seq", "exp") for stage in bits_of(axis)[::-1]]
-
-
-def spread_bits(x, order):
-    names = bit_axes()
-    x = x.reshape((2,) * len(names) + x.shape[1:])
-    tail = range(len(names), x.ndim)
-    x = jnp.transpose(x, [names.index(stage) for stage in order] + list(tail))
-    return x.reshape((2 ** len(names),) + x.shape[len(names) :])
 
 
 def collect_bits(x, order):
@@ -339,13 +449,6 @@
         (sources, set_count) + routes_row.shape
     )[:, 0, :, :token_rows]
     all_routes = jnp.transpose(all_routes, (0, 2, 1))
-    by_stream = [
-        collect_bits(part, order).reshape(sources, set_count, token_rows, width)
-        for part, order in zip(gathered, orders)
-    ]
-    all_rows = jnp.transpose(jnp.stack(by_stream, axis=3), (0, 2, 1, 3, 4)).reshape(
-        sources, token_rows, D
-    )
     expert_ids = my_block * local_experts + jnp.arange(local_experts, dtype=jnp.int32)
     member = jnp.any(all_routes[:, None] == expert_ids[None, :, None, None], axis=3).astype(jnp.int32)
     rank = jnp.cumsum(member, axis=2) - member
@@ -353,27 +456,10 @@
         rank[:, :, None, :] == jnp.arange(CAP, dtype=jnp.int32)[None, None, :, None]
     )
     chosen = chosen.astype(jnp.bfloat16)
-    picked = jnp.einsum("sect,std->escd", chosen, all_rows, preferred_element_type=jnp.float32)
-    picked = picked.astype(jnp.bfloat16).reshape(local_experts, sources * CAP, D)
     own_router = lax.dynamic_slice_in_dim(router, my_block * local_experts, local_experts, 1)
-    logits = jnp.einsum("erd,de->er", picked, own_router, preferred_element_type=jnp.float32)
-    gate_pre = jnp.einsum("erd,edf->erf", picked, gate_w, preferred_element_type=jnp.float32)
-    up_pre = jnp.einsum("erd,edf->erf", picked, up_w, preferred_element_type=jnp.float32)
-    activity = jax.nn.silu(gate_pre) * up_pre * jax.nn.sigmoid(logits)[:, :, None]
-    finished = jnp.einsum(
-        "erf,efd->erd", activity.astype(jnp.bfloat16), down_w, preferred_element_type=jnp.float32
-    ).astype(jnp.bfloat16).reshape(local_experts, sources, CAP, D)
-    combined = jnp.einsum("sect,escd->std", chosen, finished, preferred_element_type=jnp.float32)
-    combined = combined.astype(jnp.bfloat16).reshape(sources, token_rows, set_count, column_count)
-    combined = jnp.transpose(combined, (0, 2, 1, 3)).reshape(-1, token_rows, column_count)
-    summed_share = jnp.concatenate(
-        reduce_all(
-            [spread_bits(part, order) for part, order in zip(columns_cut(combined, width), orders)],
-            orders,
-            5,
-        ),
-        axis=1,
-    )
+    own_router = jnp.pad(own_router, ((0, 0), (0, 128 - local_experts)))
+    combined = expert_sums(gathered[:-1], orders, chosen, own_router, (gate_w, up_w, down_w))
+    summed_share = jnp.concatenate(reduce_all(combined, orders, 5), axis=1)
     return (
         (residual + summed_share)
         .astype(jnp.bfloat16)

time: 179 us -> 157 us (0.88)
  Pallas kernels: 101 us -> 128 us
  matrix products: 27.2 us -> 3.08 us
  local copies, waits for them, and re-layouts: 35.1 us -> 13 us
    pallas_call x5 -> x6, Pallas kernels: 101 us -> 128 us  [the longest x3 56.8 us: gather_all(): pl.pallas_call(functools.partial(gather_kernel, orders, starts_of(parts,...]
    dot_general x5 -> x0, matrix products: 24.2 us -> none  [the longest x1 13.6 us: local(): jnp.einsum('erf,efd->erd', activity.astype(jnp.bfloat16), down_w, preferr...]
    transpose x5 -> x0, local copies, waits for them, and re-layouts: 9.82 us -> none  [the longest x1 5.4 us: local(): jnp.transpose(jnp.stack(by_stream, axis=3), (0, 2, 1, 3, 4))]
    reshape x1 -> x0, local copies, waits for them, and re-layouts: 7.77 us -> none  [local(): jnp.transpose(jnp.stack(by_stream, axis=3), (0, 2, 1, 3, 4))]
    reshape x5 -> x1, local copies, waits for them, and re-layouts: 3.85 us -> 0.91 us  [collect_bits(): x = x.reshape((2,) * len(names) + x.shape[1:])]
    unnamed x31 -> x22, local copies, waits for them, and re-layouts: 5.49 us -> 4.32 us
where the time goes in v3:
time: 157 us; the launch traced here: 156 us
  Pallas kernels  128 us (82%)
  local copies, waits for them, and re-layouts  13 us (8%)
  other arithmetic  11.5 us (7%)
  matrix products  3.08 us (2%)
    pallas_call x3, Pallas kernels, gather_all(): pl.pallas_call(functools.partial(gather_kernel, orders, starts_of(parts,...  56.8 us
    pallas_call x2, Pallas kernels, reduce_all(): pl.pallas_call(functools.partial(reduce_kernel, orders, starts_of(parts,...  45.1 us
    pallas_call x1, Pallas kernels, expert_sums(): pl.pallas_call(functools.partial(expert_kernel, orders, (sources, sets, l...  25.6 us
    unnamed x22, local copies, waits for them, and re-layouts  4.32 us

profile of v3, /device:TPU:0, one launch (start us, length us, event | category | flops | bytes accessed | tf_op | source)
XLA Modules:
  0.0 156.3 jit_solution(17666279947163007709)
XLA Ops:
  0.0 0.0 copy-start
  0.7 0.7 fusion.30
  1.5 0.1 eq.127
  1.6 0.7 dynamic-slice_convert_fusion
  2.2 1.3 pad.13.refs_4_
  3.5 0.1 broadcast_reduce_fusion
  3.6 0.1 add.131
  3.7 0.1 add.133
  3.9 0.8 fusion.23
  4.7 0.2 convolution_minimum_fusion.4
  4.8 0.2 convolution_minimum_fusion.3
  5.0 0.2 convolution_minimum_fusion.2
  5.2 0.2 convolution_minimum_fusion.1
  5.3 0.2 convolution_minimum_fusion
  5.5 0.2 fusion.37
  5.7 0.1 fusion.25
  5.8 0.1 add_bitcast_fusion
  5.8 1.1 copy.82
  7.0 1.0 slice_bitcast_fusion
  8.1 0.3 copy.78
  8.4 1.0 pad.14.router_ref
  9.4 0.1 fusion.34
  9.5 0.2 copy.80
  9.6 0.2 copy.62
  9.8 0.8 fusion.36
  10.6 0.2 copy.83
  10.8 0.2 copy.59
  11.0 0.5 fusion.2
  11.5 0.4 fusion.7
  11.9 0.2 copy.65
  12.1 0.8 copy.104
  12.9 0.1 copy.66
  13.0 0.1 copy.67
  13.1 0.1 maximum_bitcast_fusion.4
  13.1 0.6 pad.12.refs_1_
  13.8 11.8 %shard_map.139 = (bf16[2,64,2048]{2,1,0:T(8,128)(2,1)}, f32[2,64,128]{2,1,0:T(8,128)}) custom-call(bf16[64,2048]{1,0:T(8,128)(2,1)} %bitcast.138, f32[64,128]{1,0:T(8,128)} %pad.12.refs_1_), custom_call_target="tpu_custom_call" | custom-call | tf_op jit(solution)/shard_map/pallas_call | solution.py:92
  25.6 0.9 fusion.29
  26.5 0.1 constant_dynamic-slice_fusion
  26.6 0.1 constant_dynamic-slice_fusion.3
  26.7 1.3 convert_bitcast_fusion.1
  28.0 0.1 copy.86
  28.1 0.1 copy.87
  28.2 0.3 fusion.17
  28.4 0.6 copy-done.1
  29.0 0.8 convolution_convert_fusion
  29.9 0.7 copy.105
  30.6 6.7 %shard_map.140 = f32[64,1024]{1,0:T(8,128)} custom-call(bf16[2,64,1024]{2,1,0:T(8,128)(2,1)} %bitcast.140), custom_call_target="tpu_custom_call" | custom-call | tf_op jit(solution)/shard_map/pallas_call | solution.py:166
  37.3 1.1 multiply_reduce_fusion
  38.4 0.7 broadcast_in_dim.43.refs_0_
  39.1 5.3 %shard_map.141 = f32[2,64,128]{2,1,0:T(8,128)} custom-call(f32[64,128]{1,0:T(8,128)} %broadcast_in_dim.43.refs_0_), custom_call_target="tpu_custom_call" | custom-call | tf_op jit(solution)/shard_map/pallas_call | solution.py:92
  44.4 0.9 slice_reduce_fusion
  45.4 1.1 multiply_convert_fusion
  46.4 0.6 fusion.35
  47.1 39.7 %shard_map.142 = (bf16[32,64,256]{2,1,0:T(8,128)(2,1)}, bf16[32,64,256]{2,1,0:T(8,128)(2,1)}, bf16[32,64,256]{2,1,0:T(8,128)(2,1)}, bf16[32,64,256]{2,1,0:T(8,128)(2,1)}, s32[32,8,128]{2,1,0:T(8,128)}) custom-call(bf16[64,256]{1,0:T(8,128)(2,1)} %get-tuple-element.44.refs_0_, bf16[64,256]{1,0:T(8,128)(2,1)} %get-tuple-element.43.refs_1_, ...), custom_call_target="tpu_custom_call" | custom-call | tf_op jit(solution)/shard_map/pallas_call | solution.py:92
  86.8 0.9 copy.69
  87.7 0.2 compare_reduce_fusion
  87.9 1.1 reduce_window_sum.11
  89.1 0.3 copy.74
  89.4 0.2 copy.73
  89.6 0.1 and_convert_fusion
  89.7 0.9 copy.76.select_ref
  90.6 25.6 %shard_map.143 = (bf16[32,64,256]{2,1,0:T(8,128)(2,1)}, bf16[32,64,256]{2,1,0:T(8,128)(2,1)}, bf16[32,64,256]{2,1,0:T(8,128)(2,1)}, bf16[32,64,256]{2,1,0:T(8,128)(2,1)}) custom-call(bf16[16,64,64]{2,1,0:T(8,128)(2,1)} %copy.76.select_ref, bf16[16,64,64]{2,1,0:T(8,128)(2,1)} %bitcast.133, bf16[2048,128]{1,0:T(8,128)(2,1)} %pad.14.router_ref, ...), custom_call_target="tpu_custom_call" | custom-call | flops 6442450944 | bytes 25165824 | tf_op jit(solution)/shard_map/pallas_call | solution.py:268
  116.2 38.4 %shard_map.144 = (f32[64,256]{1,0:T(8,128)}, f32[64,256]{1,0:T(8,128)}, f32[64,256]{1,0:T(8,128)}, f32[64,256]{1,0:T(8,128)}) custom-call(bf16[32,64,256]{2,1,0:T(8,128)(2,1)} %get-tuple-element.27.refs_0_, bf16[32,64,256]{2,1,0:T(8,128)(2,1)} %get-tuple-element.28.refs_1_, bf16[32,64,256]{2,1,0:T(8,128)(2,1)} %get-tuple-element.29.refs_2_, ...), custom_call_target="tpu_custom_call" | custom-call | tf_op jit(solution)/shard_map/pallas_call | solution.py:166
  154.7 1.6 %fusion.18 = bf16[1,64,1024]{2,1,0:T(8,128)(2,1)} fusion(f32[64,256]{1,0:T(8,128)} %get-tuple-element.34, f32[64,256]{1,0:T(8,128)} %get-tuple-element.33, f32[64,256]{1,0:T(8,128)} %get-tuple-element.32, f32[64,256]{1,0:T(8,128)} %get-tuple-element.31, f32[64,1024]{1,0:T(8,128)S(1)} %copy-done.2, bf16[1,64,2048]{2,1,0:T(8,128)(2,1)S(1)} %copy-done.5, ...), kind=kLoop, calls=%fused_computation.40 | loop fusion | flops 458752 | bytes 786436 | tf_op jit(solution)/shard_map/reshape | solution.py:466
  (29 shorter events, 0.3 us)
Async XLA Ops:
  0.0 3.8 %copy-start = (bf16[2048,64]{0,1:T(8,128)(2,1)S(1)}, bf16[2048,64]{0,1:T(8,128)(2,1)}, u32[]{:S(2)}) copy-start(bf16[2048,64]{0,1:T(8,128)(2,1)} %param.23) | copy-start | bytes 786436
  5.8 3.5 %copy-start.4 = (bf16[2,12,16,2048]{3,2,1,0:T(8,128)(2,1)S(1)}, bf16[2,12,16,2048]{3,2,1,0:T(8,128)(2,1)}, u32[]{:S(2)}) copy-start(bf16[2,12,16,2048]{3,2,1,0:T(8,128)(2,1)} %param.16) | copy-start | bytes 4718596
  26.7 2.4 %copy-start.1 = (bf16[1024,2048]{1,0:T(8,128)(2,1)S(1)}, bf16[1024,2048]{1,0:T(8,128)(2,1)}, u32[]{:S(2)}) copy-start(bf16[1024,2048]{1,0:T(8,128)(2,1)} %param.22) | copy-start | bytes 12582916
  29.0 8.3 %copy-start.5 = (bf16[1,64,2048]{2,1,0:T(8,128)(2,1)S(1)}, bf16[1,64,2048]{2,1,0:T(8,128)(2,1)}, u32[]{:S(2)}) copy-start(bf16[1,64,2048]{2,1,0:T(8,128)(2,1)} %param.20) | copy-start | bytes 786436
  89.7 0.9 copy-start.3
  116.2 38.4 %copy-start.2 = (f32[64,1024]{1,0:T(8,128)S(1)}, f32[64,1024]{1,0:T(8,128)}, u32[]{:S(2)}) copy-start(f32[64,1024]{1,0:T(8,128)} %shard_map.140) | copy-start | bytes 786436

commit v4 on v3

--- a/solution.py
+++ b/solution.py
@@ -38,7 +38,7 @@
 def starts_of(parts, steps):
     if steps < 3:
         return [0] * len(parts)
-    return [2 if i // 2 % 2 == 1 else 0 for i in range(len(parts))]
+    return [2 if i in (2, 3) else 0 for i in range(len(parts))]
 
 
 def greet(stages):
@@ -164,7 +164,7 @@
     steps = len(orders[0])
     vmem = pl.BlockSpec(memory_space=pltpu.VMEM)
     return pl.pallas_call(
-        functools.partial(reduce_kernel, orders, starts_of(parts, steps)),
+        functools.partial(reduce_kernel, orders, [0] * len(parts)),
         out_shape=[jax.ShapeDtypeStruct(part.shape[1:], jnp.float32) for part in parts],
         in_specs=[vmem] * len(parts),
         out_specs=[vmem] * len(parts),
@@ -183,7 +183,7 @@
     )(*parts)
 
 
-def expert_kernel(orders, counts, select_ref, back_ref, router_ref, *refs):
+def expert_kernel(orders, counts, select_ref, back_ref, norm_ref, router_ref, *refs):
     sources, sets, seq_count = counts
     streams, steps = len(orders), len(orders[0])
     ins = refs[:streams]
@@ -235,7 +235,9 @@
             gate_pre += jnp.dot(rows, weights[0][e, cut, :], preferred_element_type=jnp.float32)
             up_pre += jnp.dot(rows, weights[1][e, cut, :], preferred_element_type=jnp.float32)
             logits += jnp.dot(rows, router_ref[cut, :], preferred_element_type=jnp.float32)
-        activity = jax.nn.silu(gate_pre) * up_pre * jax.nn.sigmoid(logits[:, e : e + 1])
+        norm = norm_ref[e]
+        gate = jax.nn.sigmoid(logits[:, e : e + 1] * norm)
+        activity = jax.nn.silu(gate_pre * norm) * (up_pre * norm) * gate
         activity = activity.astype(jnp.bfloat16)
         for k in range(blocks):
             cut = slice(k * width, (k + 1) * width)
@@ -257,7 +259,7 @@
     lax.fori_loop(0, places, combine, 0)
 
 
-def expert_sums(parts, orders, chosen, router, weights):
+def expert_sums(parts, orders, chosen, slot_norm, router, weights):
     sources, experts, _, tokens = chosen.shape
     sets = lax.axis_size("exp")
     width = parts[0].shape[2]
@@ -268,7 +270,7 @@
     return pl.pallas_call(
         functools.partial(expert_kernel, orders, (sources, sets, lax.axis_size("seq"))),
         out_shape=[jax.ShapeDtypeStruct(part.shape, part.dtype) for part in parts],
-        in_specs=[vmem] * (3 + len(parts)) + [pl.BlockSpec(memory_space=pl.ANY)] * 3,
+        in_specs=[vmem] * (4 + len(parts)) + [pl.BlockSpec(memory_space=pl.ANY)] * 3,
         out_specs=[vmem] * len(parts),
         scratch_shapes=[pltpu.VMEM(weight.shape, weight.dtype) for weight in weights]
         + [
@@ -280,7 +282,7 @@
         cost_estimate=pl.CostEstimate(
             flops=flops, bytes_accessed=3 * weights[0].size * 2, transcendentals=0
         ),
-    )(select, jnp.swapaxes(select, 1, 2), router, *parts, *weights)
+    )(select, jnp.swapaxes(select, 1, 2), slot_norm, router, *parts, *weights)
 
 
 def bit_axes():
@@ -426,11 +428,7 @@
 
     residual = own_part(hidden.reshape(token_rows, D)).astype(jnp.float32) + projected
     own_sq = jnp.sum(residual * residual, axis=1, keepdims=True)
-    (all_sq,) = gather_all([jnp.broadcast_to(own_sq, (token_rows, 128))], [exp_bits], 3)
-    mean_sq = jnp.sum(all_sq[:, :, :1], axis=0) / D
-    normed = (
-        residual * lax.rsqrt(mean_sq + EPS_NORM) * own_part(norm_gain).astype(jnp.float32)[None, :]
-    ).astype(jnp.bfloat16)
+    weighed = (residual * own_part(norm_gain).astype(jnp.float32)[None, :]).astype(jnp.bfloat16)
     width = max(128, column_count // 4)
     streams = column_count // width
     orders = stream_orders(streams)
@@ -439,13 +437,17 @@
     routes_row = jnp.pad(
         jnp.transpose(routes.reshape(token_rows, TOPK)), ((0, 0), (0, -token_rows % 128))
     )
+    sq_row = jnp.pad(jnp.transpose(own_sq), ((0, 7), (0, -token_rows % 128)))
     gathered = gather_all(
-        columns_cut(normed, width) + [routes_row],
-        [order[::-1] for order in orders] + [orders[0][::-1]],
+        columns_cut(weighed, width) + [routes_row, sq_row],
+        [order[::-1] for order in orders] + [orders[0][::-1]] * 2,
         4,
     )
     sources = lax.axis_size("kv") * lax.axis_size("seq")
-    all_routes = collect_bits(gathered[-1], orders[0]).reshape(
+    all_sq = collect_bits(gathered[-1], orders[0]).reshape((sources, set_count) + sq_row.shape)
+    mean_sq = jnp.sum(all_sq[:, :, 0, :token_rows], axis=1) / D
+    inverse_norm = lax.rsqrt(mean_sq + EPS_NORM)
+    all_routes = collect_bits(gathered[-2], orders[0]).reshape(
         (sources, set_count) + routes_row.shape
     )[:, 0, :, :token_rows]
     all_routes = jnp.transpose(all_routes, (0, 2, 1))
@@ -455,10 +457,12 @@
     chosen = (member[:, :, None, :] > 0) & (
         rank[:, :, None, :] == jnp.arange(CAP, dtype=jnp.int32)[None, None, :, None]
     )
+    slot_norm = jnp.sum(jnp.where(chosen, inverse_norm[:, None, None, :], 0.0), axis=3)
+    slot_norm = jnp.transpose(slot_norm, (1, 0, 2)).reshape(local_experts, sources * CAP, 1)
     chosen = chosen.astype(jnp.bfloat16)
     own_router = lax.dynamic_slice_in_dim(router, my_block * local_experts, local_experts, 1)
     own_router = jnp.pad(own_router, ((0, 0), (0, 128 - local_experts)))
-    combined = expert_sums(gathered[:-1], orders, chosen, own_router, (gate_w, up_w, down_w))
+    combined = expert_sums(gathered[:-2], orders, chosen, slot_norm, own_router, (gate_w, up_w, down_w))
     summed_share = jnp.concatenate(reduce_all(combined, orders, 5), axis=1)
     return (
         (residual + summed_share)

time: 157 us -> 152 us (0.968)
  Pallas kernels: 128 us -> 123 us
  local copies, waits for them, and re-layouts: 13 us -> 15.1 us
  other arithmetic: 11.5 us -> 9.8 us
    pallas_call x3 -> x2, Pallas kernels: 56.8 us -> 51.9 us  [gather_all(): pl.pallas_call(functools.partial(gather_kernel, orders, starts_of(parts,...]
where the time goes in v4:
time: 152 us
  Pallas kernels  123 us (81%)
  local copies, waits for them, and re-layouts  15.1 us (10%)
  other arithmetic  9.8 us (6%)
  matrix products  3.08 us (2%)
    pallas_call x2, Pallas kernels, gather_all(): pl.pallas_call(functools.partial(gather_kernel, orders, starts_of(parts,...  51.9 us
    pallas_call x2, Pallas kernels, reduce_all(): pl.pallas_call(functools.partial(reduce_kernel, orders, [0] * len(parts))...  44.8 us
    pallas_call x1, Pallas kernels, expert_sums(): pl.pallas_call(functools.partial(expert_kernel, orders, (sources, sets, l...  26 us
    unnamed x22, local copies, waits for them, and re-layouts  4.32 us

profile of v4, /device:TPU:0, one launch (start us, length us, event | category | flops | bytes accessed | tf_op | source)
XLA Modules:
  0.0 151.7 jit_solution(12177620660607834154)
XLA Ops:
  0.0 0.0 copy-start
  0.7 0.7 fusion.31
  1.5 0.1 eq.131
  1.6 0.7 dynamic-slice_convert_fusion
  2.2 1.3 pad.17.refs_4_
  3.5 0.1 broadcast_reduce_fusion
  3.6 0.1 add.132
  3.7 0.1 add.134
  3.9 0.8 fusion.24
  4.6 0.2 convolution_minimum_fusion.4
  4.8 0.2 convolution_minimum_fusion.3
  5.0 0.2 convolution_minimum_fusion.2
  5.2 0.2 convolution_minimum_fusion.1
  5.3 0.2 convolution_minimum_fusion
  5.5 0.2 fusion.38
  5.7 0.1 fusion.26
  5.8 0.1 add_bitcast_fusion
  5.8 1.1 copy.90
  7.0 1.0 slice_bitcast_fusion
  8.1 0.3 copy.86
  8.4 1.0 pad.19.router_ref
  9.4 0.1 fusion.35
  9.5 0.2 copy.88
  9.6 0.2 copy.67
  9.8 0.8 fusion.37
  10.6 0.2 copy.91
  10.8 0.2 copy.64
  11.0 0.5 fusion.2
  11.5 0.4 fusion.7
  11.9 0.2 copy.70
  12.1 0.8 copy.112
  12.9 0.1 copy.71
  13.0 0.1 copy.72
  13.1 0.1 maximum_bitcast_fusion.4
  13.1 0.6 pad.16.refs_1_
  13.8 11.8 %shard_map.139 = (bf16[2,64,2048]{2,1,0:T(8,128)(2,1)}, f32[2,64,128]{2,1,0:T(8,128)}) custom-call(bf16[64,2048]{1,0:T(8,128)(2,1)} %bitcast.144, f32[64,128]{1,0:T(8,128)} %pad.16.refs_1_), custom_call_target="tpu_custom_call" | custom-call | tf_op jit(solution)/shard_map/pallas_call | solution.py:92
  25.6 0.9 fusion.30
  26.5 0.1 constant_dynamic-slice_fusion
  26.6 0.1 constant_dynamic-slice_fusion.3
  26.7 1.3 convert_bitcast_fusion.1
  28.0 0.1 copy.94
  28.1 0.1 copy.95
  28.2 0.3 fusion.18
  28.4 0.6 copy-done.1
  29.0 0.8 convolution_convert_fusion
  29.9 0.7 copy.113
  30.6 6.7 %shard_map.140 = f32[64,1024]{1,0:T(8,128)} custom-call(bf16[2,64,1024]{2,1,0:T(8,128)(2,1)} %bitcast.146), custom_call_target="tpu_custom_call" | custom-call | tf_op jit(solution)/shard_map/pallas_call | solution.py:166
  37.3 1.1 multiply_reduce_fusion
  38.4 0.6 pad.18.refs_5_
  39.0 0.6 fusion.36
  39.6 40.1 %shard_map.141 = (bf16[32,64,256]{2,1,0:T(8,128)(2,1)}, bf16[32,64,256]{2,1,0:T(8,128)(2,1)}, bf16[32,64,256]{2,1,0:T(8,128)(2,1)}, bf16[32,64,256]{2,1,0:T(8,12...) custom-call(bf16[64,256]{1,0:T(8,128)(2,1)} %get-tuple-element.48.refs_0_, ...), custom_call_target="tpu_custom_call" | custom-call | tf_op jit(solution)/shard_map/pallas_call | solution.py:92
  79.8 0.9 copy.74
  80.7 0.2 compare_reduce_fusion
  80.9 0.9 copy.80
  81.9 1.1 reduce_window_sum.11
  83.0 0.2 select_reduce_fusion
  83.3 0.3 copy.79
  83.6 1.2 reshape.428.norm_ref
  84.8 0.2 copy.78
  85.0 0.1 and_convert_fusion
  85.1 0.9 copy.83.select_ref
  86.0 26.0 %shard_map.142 = (bf16[32,64,256]{2,1,0:T(8,128)(2,1)}, bf16[32,64,256]{2,1,0:T(8,128)(2,1)}, bf16[32,64,256]{2,1,0:T(8,128)(2,1)}, bf16[32,64,256]{2,1,0:T(8,128)(2,1)}) custom-call(bf16[16,64,64]{2,1,0:T(8,128)(2,1)} %copy.83.select_ref, bf16[16,64,64]{2,1,0:T(8,128)(2,1)} %bitcast.139, f32[4,256,1]{2,1,0:T(8,128)} %reshape.428.norm_ref, ...), custom_call_target="tpu_custom_call" | custom-call | flops 6442450944 | bytes 25165824 | tf_op jit(solution)/shard_map/pallas_call | solution.py:270
  112.0 38.1 %shard_map.143 = (f32[64,256]{1,0:T(8,128)}, f32[64,256]{1,0:T(8,128)}, f32[64,256]{1,0:T(8,128)}, f32[64,256]{1,0:T(8,128)}) custom-call(bf16[32,64,256]{2,1,0:T(8,128)(2,1)} %get-tuple-element.29.refs_0_, bf16[32,64,256]{2,1,0:T(8,128)(2,1)} %get-tuple-element.30.refs_1_, bf16[32,64,256]{2,1,0:T(8,128)(2,1)} %get-tuple-element.31.refs_2_, ...), custom_call_target="tpu_custom_call" | custom-call | tf_op jit(solution)/shard_map/pallas_call | solution.py:166
  150.1 1.6 %fusion.19 = bf16[1,64,1024]{2,1,0:T(8,128)(2,1)} fusion(f32[64,256]{1,0:T(8,128)} %get-tuple-element.36, f32[64,256]{1,0:T(8,128)} %get-tuple-element.35, f32[64,256]{1,0:T(8,128)} %get-tuple-element.34, f32[64,256]{1,0:T(8,128)} %get-tuple-element.33, f32[64,1024]{1,0:T(8,128)S(1)} %copy-done.3, bf16[1,64,2048]{2,1,0:T(8,128)(2,1)S(1)} %copy-done.5, ...), kind=kLoop, calls=%fused_computation.43 | loop fusion | flops 458752 | bytes 786436 | tf_op jit(solution)/shard_map/reshape | solution.py:470
  (31 shorter events, 0.4 us)
Async XLA Ops:
  0.0 3.8 %copy-start = (bf16[2048,64]{0,1:T(8,128)(2,1)S(1)}, bf16[2048,64]{0,1:T(8,128)(2,1)}, u32[]{:S(2)}) copy-start(bf16[2048,64]{0,1:T(8,128)(2,1)} %param.23) | copy-start | bytes 786436
  5.8 3.5 %copy-start.4 = (bf16[2,12,16,2048]{3,2,1,0:T(8,128)(2,1)S(1)}, bf16[2,12,16,2048]{3,2,1,0:T(8,128)(2,1)}, u32[]{:S(2)}) copy-start(bf16[2,12,16,2048]{3,2,1,0:T(8,128)(2,1)} %param.16) | copy-start | bytes 4718596
  26.7 2.4 %copy-start.1 = (bf16[1024,2048]{1,0:T(8,128)(2,1)S(1)}, bf16[1024,2048]{1,0:T(8,128)(2,1)}, u32[]{:S(2)}) copy-start(bf16[1024,2048]{1,0:T(8,128)(2,1)} %param.22) | copy-start | bytes 12582916
  29.0 8.3 %copy-start.5 = (bf16[1,64,2048]{2,1,0:T(8,128)(2,1)S(1)}, bf16[1,64,2048]{2,1,0:T(8,128)(2,1)}, u32[]{:S(2)}) copy-start(bf16[1,64,2048]{2,1,0:T(8,128)(2,1)} %param.20) | copy-start | bytes 786436
  85.1 0.9 copy-start.2
  112.0 38.1 %copy-start.3 = (f32[64,1024]{1,0:T(8,128)S(1)}, f32[64,1024]{1,0:T(8,128)}, u32[]{:S(2)}) copy-start(f32[64,1024]{1,0:T(8,128)} %shard_map.140) | copy-start | bytes 786436

commit v5 on v4

--- a/solution.py
+++ b/solution.py
@@ -212,6 +212,14 @@
                 source = source + value * 2**bit * (seq_count if axis == "kv" else 1)
         return source, column_set
 
+    def in_fours(body):
+        def four(quarter, carry):
+            for step in range(4):
+                carry = body(quarter * 4 + step, carry)
+            return carry
+
+        lax.fori_loop(0, places // 4, four, 0)
+
     def pick(p, carry):
         for i, order in enumerate(orders):
             source, column_set = whose(order, p)
@@ -223,7 +231,7 @@
                 ] = rows[e * CAP : (e + 1) * CAP]
         return carry
 
-    lax.fori_loop(0, places, pick, 0)
+    in_fours(pick)
     blocks = sets * streams
     for e in range(experts):
         for j in range(3):
@@ -256,7 +264,7 @@
             ).astype(jnp.bfloat16)
         return carry
 
-    lax.fori_loop(0, places, combine, 0)
+    in_fours(combine)
 
 
 def expert_sums(parts, orders, chosen, slot_norm, router, weights):

time: 152 us -> 145 us (0.954)
  Pallas kernels: 123 us -> 116 us
    pallas_call x1, Pallas kernels: 26 us -> 19.1 us  [expert_sums(): pl.pallas_call(functools.partial(expert_kernel, orders, (sources, sets, l...]
where the time goes in v5:
time: 145 us
  Pallas kernels  116 us (80%)
  local copies, waits for them, and re-layouts  15.1 us (10%)
  other arithmetic  9.8 us (7%)
  matrix products  3.08 us (2%)
    pallas_call x2, Pallas kernels, gather_all(): pl.pallas_call(functools.partial(gather_kernel, orders, starts_of(parts,...  51.9 us
    pallas_call x2, Pallas kernels, reduce_all(): pl.pallas_call(functools.partial(reduce_kernel, orders, [0] * len(parts))...  44.8 us
    pallas_call x1, Pallas kernels, expert_sums(): pl.pallas_call(functools.partial(expert_kernel, orders, (sources, sets, l...  19.1 us
    unnamed x22, local copies, waits for them, and re-layouts  4.32 us

profile of v5, /device:TPU:0, one launch (start us, length us, event | category | flops | bytes accessed | tf_op | source)
XLA Modules:
  0.0 144.8 jit_solution(1182712580749087414)
XLA Ops:
  0.7 0.7 fusion.31
  1.5 0.1 eq.131
  1.6 0.7 dynamic-slice_convert_fusion
  2.2 1.3 pad.17.refs_4_
  3.5 0.1 broadcast_reduce_fusion
  3.6 0.1 add.132
  3.7 0.1 add.134
  3.9 0.8 fusion.24
  4.6 0.2 convolution_minimum_fusion.4
  4.8 0.2 convolution_minimum_fusion.3
  5.0 0.2 convolution_minimum_fusion.2
  5.2 0.2 convolution_minimum_fusion.1
  5.3 0.2 convolution_minimum_fusion
  5.5 0.2 fusion.38
  5.7 0.1 fusion.26
  5.8 0.1 add_bitcast_fusion
  5.8 1.1 copy.90
  7.0 1.0 slice_bitcast_fusion
  8.1 0.3 copy.86
  8.4 1.0 pad.19.router_ref
  9.4 0.1 fusion.35
  9.5 0.2 copy.88
  9.6 0.2 copy.67
  9.8 0.8 fusion.37
  10.6 0.2 copy.91
  10.8 0.2 copy.64
  11.0 0.5 fusion.2
  11.5 0.4 fusion.7
  11.9 0.2 copy.70
  12.1 0.8 copy.112
  12.9 0.1 copy.71
  13.0 0.1 copy.72
  13.1 0.1 maximum_bitcast_fusion.4
  13.1 0.6 pad.16.refs_1_
  13.8 11.8 %shard_map.139 = (bf16[2,64,2048]{2,1,0:T(8,128)(2,1)}, f32[2,64,128]{2,1,0:T(8,128)}) custom-call(bf16[64,2048]{1,0:T(8,128)(2,1)} %bitcast.144, f32[64,128]{1,0:T(8,128)} %pad.16.refs_1_), custom_call_target="tpu_custom_call" | custom-call | tf_op jit(solution)/shard_map/pallas_call | solution.py:92
  25.6 0.9 fusion.30
  26.5 0.1 constant_dynamic-slice_fusion
  26.6 0.1 constant_dynamic-slice_fusion.3
  26.7 1.3 convert_bitcast_fusion.1
  28.0 0.1 copy.94
  28.1 0.1 copy.95
  28.2 0.3 fusion.18
  28.4 0.6 copy-done.1
  29.0 0.8 convolution_convert_fusion
  29.9 0.7 copy.113
  30.6 6.7 %shard_map.140 = f32[64,1024]{1,0:T(8,128)} custom-call(bf16[2,64,1024]{2,1,0:T(8,128)(2,1)} %bitcast.146), custom_call_target="tpu_custom_call" | custom-call | tf_op jit(solution)/shard_map/pallas_call | solution.py:166
  37.3 1.1 multiply_reduce_fusion
  38.4 0.6 pad.18.refs_5_
  39.0 0.6 fusion.36
  39.6 40.1 %shard_map.141 = (bf16[32,64,256]{2,1,0:T(8,128)(2,1)}, bf16[32,64,256]{2,1,0:T(8,128)(2,1)}, bf16[32,64,256]{2,1,0:T(8,128)(2,1)}, bf16[32,64,256]{2,1,0:T(8,12...) custom-call(bf16[64,256]{1,0:T(8,128)(2,1)} %get-tuple-element.48.refs_0_, ...), custom_call_target="tpu_custom_call" | custom-call | tf_op jit(solution)/shard_map/pallas_call | solution.py:92
  79.8 0.9 copy.74
  80.7 0.2 compare_reduce_fusion
  80.9 0.9 copy.80
  81.9 1.1 reduce_window_sum.11
  83.0 0.2 select_reduce_fusion
  83.3 0.3 copy.79
  83.6 1.2 reshape.428.norm_ref
  84.8 0.2 copy.78
  85.0 0.1 and_convert_fusion
  85.1 0.9 copy.83.select_ref
  86.0 19.1 %shard_map.142 = (bf16[32,64,256]{2,1,0:T(8,128)(2,1)}, bf16[32,64,256]{2,1,0:T(8,128)(2,1)}, bf16[32,64,256]{2,1,0:T(8,128)(2,1)}, bf16[32,64,256]{2,1,0:T(8,128)(2,1)}) custom-call(bf16[16,64,64]{2,1,0:T(8,128)(2,1)} %copy.83.select_ref, bf16[16,64,64]{2,1,0:T(8,128)(2,1)} %bitcast.139, f32[4,256,1]{2,1,0:T(8,128)} %reshape.428.norm_ref, ...), custom_call_target="tpu_custom_call" | custom-call | flops 6442450944 | bytes 25165824 | tf_op jit(solution)/shard_map/pallas_call | solution.py:278
  105.1 38.1 %shard_map.143 = (f32[64,256]{1,0:T(8,128)}, f32[64,256]{1,0:T(8,128)}, f32[64,256]{1,0:T(8,128)}, f32[64,256]{1,0:T(8,128)}) custom-call(bf16[32,64,256]{2,1,0:T(8,128)(2,1)} %get-tuple-element.29.refs_0_, bf16[32,64,256]{2,1,0:T(8,128)(2,1)} %get-tuple-element.30.refs_1_, bf16[32,64,256]{2,1,0:T(8,128)(2,1)} %get-tuple-element.31.refs_2_, ...), custom_call_target="tpu_custom_call" | custom-call | tf_op jit(solution)/shard_map/pallas_call | solution.py:166
  143.2 0.0 copy-done.3
  143.2 1.6 %fusion.19 = bf16[1,64,1024]{2,1,0:T(8,128)(2,1)} fusion(f32[64,256]{1,0:T(8,128)} %get-tuple-element.36, f32[64,256]{1,0:T(8,128)} %get-tuple-element.35, f32[64,256]{1,0:T(8,128)} %get-tuple-element.34, f32[64,256]{1,0:T(8,128)} %get-tuple-element.33, f32[64,1024]{1,0:T(8,128)S(1)} %copy-done.3, bf16[1,64,2048]{2,1,0:T(8,128)(2,1)S(1)} %copy-done.5, ...), kind=kLoop, calls=%fused_computation.43 | loop fusion | flops 458752 | bytes 786436 | tf_op jit(solution)/shard_map/reshape | solution.py:478
  (31 shorter events, 0.4 us)
Async XLA Ops:
  0.0 3.8 %copy-start = (bf16[2048,64]{0,1:T(8,128)(2,1)S(1)}, bf16[2048,64]{0,1:T(8,128)(2,1)}, u32[]{:S(2)}) copy-start(bf16[2048,64]{0,1:T(8,128)(2,1)} %param.23) | copy-start | bytes 786436
  5.8 3.5 %copy-start.4 = (bf16[2,12,16,2048]{3,2,1,0:T(8,128)(2,1)S(1)}, bf16[2,12,16,2048]{3,2,1,0:T(8,128)(2,1)}, u32[]{:S(2)}) copy-start(bf16[2,12,16,2048]{3,2,1,0:T(8,128)(2,1)} %param.16) | copy-start | bytes 4718596
  26.7 2.4 %copy-start.1 = (bf16[1024,2048]{1,0:T(8,128)(2,1)S(1)}, bf16[1024,2048]{1,0:T(8,128)(2,1)}, u32[]{:S(2)}) copy-start(bf16[1024,2048]{1,0:T(8,128)(2,1)} %param.22) | copy-start | bytes 12582916
  29.0 8.3 %copy-start.5 = (bf16[1,64,2048]{2,1,0:T(8,128)(2,1)S(1)}, bf16[1,64,2048]{2,1,0:T(8,128)(2,1)}, u32[]{:S(2)}) copy-start(bf16[1,64,2048]{2,1,0:T(8,128)(2,1)} %param.20) | copy-start | bytes 786436
  85.1 0.9 copy-start.2
  105.1 38.1 %copy-start.3 = (f32[64,1024]{1,0:T(8,128)S(1)}, f32[64,1024]{1,0:T(8,128)}, u32[]{:S(2)}) copy-start(f32[64,1024]{1,0:T(8,128)} %shard_map.140) | copy-start | bytes 786436
